TPU v7x, 32 devices: a whole 2x2x4 slice. The times are simulated.
32 devices in a mesh: section: 2 (over y), seq: 8 (over z, x), mp: 2 (over core).
Axes of the slice: x: 2, y: 2, z: 4, core: 2. Of those that a mesh axis runs over, the one named last changes fastest.
Arguments:
- hidden: bfloat16 [1024, 4096], P('seq'), may hold values from -6 to 6
- hidden_gain: bfloat16 [4096], replicated, may hold values from 0.5 to 1.5
- neighbour_states: bfloat16 [128, 128, 896], P('seq'), may hold values from -6 to 6
- encoder_gain: bfloat16 [896], replicated, may hold values from 0.5 to 1.5
- query_weight: bfloat16 [4096, 2048], P('section', 'mp'), may hold values from -0.09375 to 0.09375
- kv_weight: bfloat16 [2, 896, 2048], P(None, None, 'mp'), may hold values from -0.1875 to 0.1875
- attn_grad: bfloat16 [1024, 2048], P('seq', 'mp'), may hold values from -6 to 6
- neighbour_ids: int32 [16, 16], P('seq'), may hold values from 0 to 15, each once within a row
- valid_counts: int32 [16], P('seq'), may hold values from 2 to 16
Outputs:
- hidden_grad: bfloat16 [1024, 4096], P('seq', ('section', 'mp'))
- query_weight_grad: float32 [4096, 2048], P(('section', 'seq'), 'mp')
- kv_weight_grad: float32 [2, 896, 2048], P(None, ('section', 'seq'), 'mp')
- norm_dot: float32 [1024], P('seq')
Inputs may be any that keep to these rules, and one draw needn't show every extreme that they name: `neighbour_ids`: each row lists every one of the 16 pool blocks of its group once.
All inputs are finite; a program needn't handle non-finite values.
Results may differ from a plain program's by a relative error of at most 0.012.
Values may be sent and summed in bfloat16 or wider, within the bound.
No kernel may reach another device: no remote copies, remote signals or barrier semaphores. Data moves between devices by JAX's collectives and lax.ppermute only.
A program may use at most 128 MiB of HBM per device.

v0:
```python
import functools
import math

import jax
import jax.numpy as jnp
from jax import lax
from jax.experimental import pallas as pl
from jax.experimental.pallas import tpu as pltpu
from jax.sharding import PartitionSpec as P

HD = 128
EPSILON = 1e-06
MASKED = -1e30
LOG2_E = math.log2(math.e)
VMEM_BYTES = 24 * 1024 * 1024
CHUNKS = 2
NORM_FLOPS = 3_000_000_000
FIRST_ATTEND_FLOPS = 4_000_000_000
OUTER_FLOPS = 80_000_000
OWN_FLOPS = 2_000_000_000
ODD_FLOPS = 1_000_000_000

F32 = jnp.float32
BF16 = jnp.bfloat16

IN_VMEM = pl.BlockSpec(memory_space=pltpu.VMEM)
IN_SMEM = pl.BlockSpec(memory_space=pltpu.SMEM)
IN_HBM = pl.BlockSpec(memory_space=pltpu.HBM)


def shape(dims, kind):
    return jax.ShapeDtypeStruct(dims, kind)


def call(
    kernel, name, out_shape, operands, in_specs=None, scratch=(), flops=0, limit=VMEM_BYTES
):
    return pl.pallas_call(
        kernel,
        in_specs=in_specs or [IN_VMEM] * len(operands),
        out_specs=[IN_VMEM] * len(out_shape),
        out_shape=out_shape,
        scratch_shapes=scratch,
        compiler_params=pltpu.CompilerParams(vmem_limit_bytes=limit),
        cost_estimate=pl.CostEstimate(flops=flops, bytes_accessed=0, transcendentals=0),
        name=name,
    )(*operands)


def nt_dot(left, right):
    return lax.dot_general(left, right, (((1,), (1,)), ((), ())), preferred_element_type=F32)


def swapped(array, axis, mask):
    size = lax.axis_size(axis)
    return lax.ppermute(array, axis, [(i, i ^ mask) for i in range(size)])


def after(value, *others):
    return lax.optimization_barrier((value, *others))[0]


def lanes_at(ref, start, size):
    return ref[:, pl.ds(pl.multiple_of(start, size), size)]


def split_column(column):
    high = column.astype(BF16).astype(F32)
    rest = column - high
    middle = rest.astype(BF16).astype(F32)
    low = rest - middle
    lane = lax.broadcasted_iota(jnp.int32, (column.shape[0], HD), 1)
    terms = jnp.where(lane == 0, high, jnp.where(lane == 1, middle, jnp.where(lane == 2, low, 0.0)))
    return terms.astype(BF16)


def joined_column(terms):
    return jnp.sum(terms.astype(F32), axis=1, keepdims=True)


def norm_kernel(
    gain, hidden, hn, rms_out, hidden_part, gain_part, keep_out, send_out, gain_row, turned
):
    core = lax.axis_index("mp")
    width = hidden.shape[1]
    half = width // 2
    quarter = hidden_part.shape[1]
    gain_row[...] = gain[...].astype(F32).reshape(1, width)
    wide = hidden[...].astype(F32)
    inv_rms = lax.rsqrt(jnp.mean(wide * wide, axis=1, keepdims=True) + EPSILON)
    rms_out[...] = inv_rms
    hn[...] = (wide * inv_rms * gain_row[...]).astype(BF16)
    turned[...] = lanes_at(hn, core * half, half).T
    count, span = keep_out.shape[1:3]
    outer = lax.axis_index("seq") // 2
    for out, base in ((keep_out, 0), (send_out, count)):
        for step in range(count):
            start = pl.multiple_of((outer ^ (base + step)) * span, span)
            out[0, step] = turned[pl.ds(start, span), :]
    own = (2 * lax.axis_index("section") + core) * quarter
    hidden_part[...] = lanes_at(hidden, own, quarter)
    gain_part[...] = lanes_at(gain_row, own, quarter)


def norm_columns(hidden, gain, count):
    rows, width = hidden.shape
    half, quarter = width // 2, width // 4
    dims = (1, count // 2, half // count, rows)
    return call(
        norm_kernel,
        "norm_columns",
        [
            shape((rows, width), BF16),
            shape((rows, 1), F32),
            shape((rows, quarter), BF16),
            shape((1, quarter), F32),
            shape(dims, BF16),
            shape(dims, BF16),
        ],
        [gain, hidden],
        None,
        [pltpu.VMEM((1, width), F32), pltpu.VMEM((half, rows), BF16)],
        NORM_FLOPS,
    )


def query_kernel(hn, weight, grads, keep_out, send_out, pair_out, cross_out, total):
    section = lax.axis_index("section")
    half = weight.shape[0]
    lead = cross_out.shape[0]
    cols = keep_out.shape[1]
    total[...] = jnp.dot(
        lanes_at(hn, section * half, half), weight[...], preferred_element_type=F32
    )
    keep_out[...] = lanes_at(total, section * cols, cols)
    send_out[...] = lanes_at(total, (1 - section) * cols, cols).astype(BF16)
    pair_out[0] = keep_out[:lead].astype(BF16)
    pair_out[1] = grads[:lead, pl.ds(pl.multiple_of(section * cols, cols), cols)]
    cross_out[...] = send_out[:lead]


def query_part(hn, weight, attn_grad, lead):
    rows = hn.shape[0]
    local = weight.shape[1]
    cols = local // 2
    return call(
        query_kernel,
        "query_part",
        [
            shape((rows, cols), F32),
            shape((rows, cols), BF16),
            shape((2, lead, cols), BF16),
            shape((lead, cols), BF16),
        ],
        [hn, weight, attn_grad],
        None,
        [pltpu.VMEM((rows, local), F32)],
    )


def regroup_kernel(kept, received, keep_out, send_out):
    sources = kept.shape[0]
    count = keep_out.shape[1]
    for ref, place in ((kept, 0), (received, sources)):
        keep_out[place : place + sources] = ref[:, :count]
        send_out[place : place + sources] = ref[:, count:]


def columns_exchange(kept, received, count):
    bit = count // 2
    while bit > 1:
        sources, targets, *dims = kept.shape
        dims = (2 * sources, targets // 2, *dims)
        kept, send = call(
            regroup_kernel, "regroup", [shape(dims, BF16)] * 2, [kept, received]
        )
        bit //= 2
        received = swapped(send, "seq", 2 * bit)
    return kept, received


def pool_kernel(gain, states, weight, kv_out, turned_out):
    rows, width = states.shape
    cols = kv_out.shape[2]
    block = min(rows, 1024)
    start = pl.multiple_of(lax.axis_index("section") * cols, cols)
    gain_row = gain[...].astype(F32).reshape(1, width)
    for base in range(0, rows, block):
        part = slice(base, base + block)
        wide = states[part].astype(F32)
        inv_rms = lax.rsqrt(jnp.mean(wide * wide, axis=1, keepdims=True) + EPSILON)
        normed = (wide * inv_rms * gain_row).astype(BF16)
        for which in range(2):
            kv_out[which, part] = jnp.dot(
                normed, weight[which, :, pl.ds(start, cols)], preferred_element_type=F32
            ).astype(BF16)
        turned_out[:, part] = normed.T


def pool_project(states, gain, weight):
    rows, width = states.shape
    cols = weight.shape[2] // 2
    return call(
        pool_kernel,
        "pool_project",
        [shape((2, rows, cols), BF16), shape((width, rows), BF16)],
        [gain, states, weight],
    )


def rows_at(ref, start, size):
    if size % 8 == 0:
        return ref[pl.ds(pl.multiple_of(start, 8), size), :]
    window = (size + 14) // 8 * 8
    rest = start % 8
    wide = ref[pl.ds(pl.multiple_of(start - rest, 8), window), :]
    return pltpu.roll(wide, window - rest, 0)[:size]


def attend_kernel(
    chunk, slot_count, ids, counts, keep, other, pair, cross, grad_own, kv, *rest
):
    last = chunk == CHUNKS - 1
    if chunk > 0:
        before, dots_before, *rest = rest
    dq_out, dots_out, *rest = rest
    if last:
        lead_out, *rest = rest
    turned_kv, bias = rest
    section = lax.axis_index("section")
    rows, all_cols = keep.shape
    cols = all_cols // CHUNKS
    left = chunk * cols
    here = slice(left, left + cols)
    lead = cross.shape[0]
    keys = kv.shape[1]
    block_count = counts.shape[0]
    block_len = rows // block_count
    offset = block_len - 1
    length = keys // slot_count
    factor = 1.0 / math.sqrt(HD)
    slot_of = lax.broadcasted_iota(jnp.int32, (1, keys), 1) // length
    for block in range(block_count):
        line = jnp.full((1, keys), MASKED, F32)
        for slot in range(slot_count):
            opened = jnp.where(slot < counts[block], ids[block, slot], -1)
            line = jnp.where(slot_of == opened, 0.0, line)
        bias[block * block_len : (block + 1) * block_len, :] = jnp.broadcast_to(
            line, (block_len, keys)
        )
    following = lax.broadcasted_iota(jnp.int32, (rows, 1), 0) < offset
    own = keep[:, here] + other[:, here].astype(F32)
    led = pair[0, :, here].astype(F32) + cross[:, here].astype(F32)
    padding = jnp.zeros((rows - lead, cols), F32)
    queries = jnp.where(following, jnp.concatenate([led, padding], 0), own)
    own = lanes_at(grad_own, section * all_cols + left, cols).astype(F32)
    led = pair[1, :, here].astype(F32)
    grads = jnp.where(following, jnp.concatenate([led, padding], 0), own)
    rolled_queries = pltpu.roll(queries, rows - offset, 0)
    rolled_grads = pltpu.roll(grads, rows - offset, 0)
    dots = dots_before[...] if chunk > 0 else jnp.zeros((rows, 1), F32)
    if chunk > 0:
        dq_out[:, :left] = before[...]
    for head in range(cols // HD):
        span = slice(head * HD, (head + 1) * HD)
        at = slice(left + head * HD, left + (head + 1) * HD)
        query = rolled_queries[:, span].astype(BF16)
        grad = rolled_grads[:, span].astype(BF16)
        key = kv[0, :, at]
        value = kv[1, :, at]
        scores = nt_dot(query, key) * (factor * LOG2_E) + bias[...]
        peak = jnp.max(scores, axis=1, keepdims=True)
        weights = jnp.exp2(scores - peak)
        norm = 1.0 / jnp.sum(weights, axis=1, keepdims=True)
        grad_probs = nt_dot(grad, value)
        delta = jnp.sum(weights * grad_probs, axis=1, keepdims=True) * norm
        grad_scores = (weights * (grad_probs - delta)).astype(BF16)
        scale = norm * factor
        dq = jnp.dot(grad_scores, key, preferred_element_type=F32) * scale
        dq = pltpu.roll(dq, offset, 0).astype(BF16)
        dots = dots + jnp.sum(dq.astype(F32) * queries[:, span], axis=1, keepdims=True)
        dq_out[:, at] = dq
        turned_query = (query.astype(F32) * scale).T.astype(BF16)
        turned_grad = (rolled_grads[:, span] * norm).T.astype(BF16)
        turned_kv[span, :] = jnp.dot(
            turned_query, grad_scores, preferred_element_type=F32
        ).astype(BF16)
        turned_kv[cols + head * HD : cols + (head + 1) * HD, :] = jnp.dot(
            turned_grad, weights.astype(BF16), preferred_element_type=F32
        ).astype(BF16)
    if last:
        dots_out[...] = split_column(dots)
        lead_out[:, :all_cols] = dq_out[:lead]
        lead_out[:, all_cols:] = dots_out[:lead]
    else:
        dots_out[...] = dots


def kv_part_kernel(groups, turned, turned_kv, *rest):
    *outs, product = rest
    outer, inner_own = lax.axis_index("seq") // 2, lax.axis_index("seq") % 2
    width = turned.shape[0]
    product[:width] = nt_dot(turned[...], turned_kv[...])
    piece = outs[0].shape[2]
    half = width // 2
    for place, steps in enumerate(groups):
        for index, step in enumerate(steps):
            for part in range(2):
                for out, inner in ((outs[2 * place], 1 - inner_own), (outs[2 * place + 1], inner_own)):
                    start = part * half + (2 * (outer ^ step) + inner) * piece
                    out[index, part] = rows_at(product, start, piece).astype(out.dtype)


def attend(chunk, ids, counts, keep, other, pair, cross, attn_grad, kv, before):
    rows, all_cols = keep.shape
    cols = all_cols // CHUNKS
    lead = cross.shape[0]
    keys = kv.shape[1]
    last = chunk == CHUNKS - 1
    operands = [ids, counts, keep, other, pair, cross, attn_grad, kv, *before]
    out_shape = [
        shape((rows, (chunk + 1) * cols), BF16),
        shape((rows, HD), BF16) if last else shape((rows, 1), F32),
    ]
    if last:
        out_shape.append(shape((lead, all_cols + HD), BF16))
    out_shape.append(shape((2 * cols, keys), BF16))
    return call(
        functools.partial(attend_kernel, chunk, ids.shape[1]),
        "attend_%d" % chunk,
        out_shape,
        operands,
        [IN_SMEM] * 2 + [IN_VMEM] * (len(operands) - 2),
        [pltpu.VMEM((rows, keys), F32)],
        0 if last else FIRST_ATTEND_FLOPS,
    )


def kv_part(chunk, turned, turned_kv, groups):
    width = turned.shape[0]
    cols = turned_kv.shape[0]
    dims = (2, width // (2 * lax.axis_size("seq")), cols)
    return call(
        functools.partial(kv_part_kernel, groups),
        "kv_part_%d" % chunk,
        [shape((len(steps), *dims), kind) for steps in groups for kind in (BF16, F32)],
        [turned, turned_kv],
        None,
        [pltpu.VMEM((width + 16, cols), F32)],
    )


def own_kernel(offset, dq, dots, carried, out, grads_out):
    lead = carried.shape[0]
    cols = dq.shape[1]
    early = lax.broadcasted_iota(jnp.int32, (lead, 1), 0) < offset
    out[:lead, :cols] = jnp.where(early, carried[:, :cols], dq[:lead])
    out[:lead, cols:] = jnp.where(early, carried[:, cols:], dots[:lead])
    out[lead:, :cols] = dq[lead:]
    out[lead:, cols:] = dots[lead:]
    grads_out[0] = out[:, :cols]


def odd_kernel(first, first_in, second, second_in, out):
    for place in range(out.shape[1]):
        odd = 2 * place + 1
        out[0, place] = (first[odd] + first_in[odd].astype(F32)).astype(BF16)
        out[1, place] = (second[place] + second_in[place].astype(F32)).astype(BF16)


def even_kernel(first, first_in, second, second_in, out):
    for place in range(out.shape[1]):
        even = 2 * place
        out[0, place] = first[even] + first_in[even].astype(F32)
        out[1, place] = second[place] + second_in[place].astype(F32)


def both_chunks(kernel, name, kind, flops, *refs):
    dims = (CHUNKS, *refs[2].shape)
    return call(kernel, name, [shape(dims, kind)], list(refs), flops=flops)[0]


def fold_kernel(kept, received, keep_out, send_out):
    for place in range(keep_out.shape[1]):
        even, odd = 2 * place, 2 * place + 1
        keep_out[:, place] = kept[:, even] + received[:, even].astype(F32)
        send_out[:, place] = (kept[:, odd] + received[:, odd].astype(F32)).astype(BF16)


def fold(kept, received):
    chunks, count, *dims = kept.shape
    half = (chunks, count // 2, *dims)
    return call(fold_kernel, "fold", [shape(half, F32), shape(half, BF16)], [kept, received])


def outer_kernel(kept, received, mine, next_out, side_out, cross_out):
    section = lax.axis_index("section")
    for chunk in range(CHUNKS):
        for out, place, part in (
            (next_out, 1, section),
            (cross_out, 1, 1 - section),
            (side_out, 0, 1 - section),
            (mine, 0, section),
        ):
            total = kept[chunk, place, part] + received[chunk, place, part].astype(F32)
            out[chunk] = total.astype(out.dtype)


def outer_sums(kept, received):
    _, _, _, piece, cols = kept.shape
    dims = (CHUNKS, piece, cols)
    return call(
        outer_kernel, "outer_sums", [shape(dims, F32)] + [shape(dims, BF16)] * 3,
        [kept, received], flops=OUTER_FLOPS,
    )


def kv_grad_kernel(mine, following, side, cross, out):
    section = lax.axis_index("section")
    cols = mine.shape[2] // 2
    for chunk in range(CHUNKS):
        for which in range(2):
            span = slice(which * cols, (which + 1) * cols)
            own = mine[chunk, :, span] + following[chunk, :, span].astype(F32)
            other = side[chunk, :, span].astype(F32) + cross[chunk, :, span].astype(F32)
            for value, part in ((own, section), (other, 1 - section)):
                start = pl.multiple_of((part * CHUNKS + chunk) * cols, cols)
                out[which, :, pl.ds(start, cols)] = value


def weight_kernel(*refs):
    *refs, keep_out, pair_out, side_out, cross_out = refs
    mine, theirs, grads = refs[:2], refs[2:4], refs[4:]
    section = lax.axis_index("section")
    inner_own = lax.axis_index("seq") % 2
    swap = lax.axis_index("mp") != section
    piece = keep_out.shape[0]
    gathered = [ref[index] for ref in grads for index in range(ref.shape[0])]
    half = len(gathered) // 2
    for outs, inner, other in (
        (pair_out, 1 - inner_own, False),
        (cross_out, 1 - inner_own, True),
        (side_out, inner_own, True),
        (keep_out, inner_own, False),
    ):
        rows = pl.ds(pl.multiple_of(inner * piece, piece), piece)
        total = None
        for place, grad in enumerate(gathered):
            same, opposite = (refs[place // half][place % half, 0, rows, :] for refs in (mine, theirs))
            if other:
                same, opposite = opposite, same
            column = jnp.where(swap, opposite, same)
            term = jnp.dot(column, grad, preferred_element_type=F32)
            total = term if total is None else total + term
        outs[...] = total.astype(outs.dtype)


def weight_part(mine, theirs, grads):
    dims = (mine[0].shape[2] // 2, grads[0].shape[2])
    return call(
        weight_kernel,
        "weight_part",
        [shape(dims, F32)] + [shape(dims, BF16)] * 3,
        [*mine, *theirs, *grads],
    )


def stack_kernel(*refs):
    *refs, out = refs
    start = 0
    for ref in refs:
        out[start : start + ref.shape[0]] = ref[...]
        start += ref.shape[0]


def outer_gather(piece, count, ahead):
    stages, whole = [piece], piece
    bit = count // 2
    while bit:
        if len(stages) > 1:
            whole = call(
                stack_kernel,
                "stacked",
                [shape((2 * whole.shape[0], *piece.shape[1:]), BF16)],
                [after(stages[0], *ahead), *stages[1:]],
            )[0]
        stages.append(swapped(whole, "seq", 2 * bit))
        bit //= 2
    return stages


def query_grad_kernel(kept, paired, side, cross, out):
    section = lax.axis_index("section")
    cols = kept.shape[1]
    own = pl.ds(pl.multiple_of(section * cols, cols), cols)
    out[:, own] = kept[...] + paired[...].astype(F32)
    other = pl.ds(pl.multiple_of((1 - section) * cols, cols), cols)
    out[:, other] = side[...].astype(F32) + cross[...].astype(F32)


def normed_kernel(own, other, weight, keep_out, dots_out, send_out, total):
    cols = own.shape[1] - HD
    swap = lax.axis_index("section") == 1
    core = lax.axis_index("mp")
    quarter = keep_out.shape[1]
    first = jnp.where(swap, other[:, :cols], own[:, :cols])
    second = jnp.where(swap, own[:, :cols], other[:, :cols])
    total[...] = nt_dot(first, weight[:, :cols]) + nt_dot(second, weight[:, cols:])
    keep_out[...] = lanes_at(total, core * quarter, quarter)
    send_out[:, :quarter] = lanes_at(total, (1 - core) * quarter, quarter).astype(BF16)
    dots = joined_column(own[:, cols:]) + joined_column(other[:, cols:])
    dots_out[...] = dots
    send_out[:, quarter:] = split_column(dots)


def normed_part(own, other, weight):
    rows = own.shape[0]
    half = weight.shape[0]
    quarter = half // 2
    return call(
        normed_kernel,
        "normed_part",
        [shape((rows, quarter), F32), shape((rows, 1), F32), shape((rows, quarter + HD), BF16)],
        [own, other, weight],
        None,
        [pltpu.VMEM((rows, half), F32)],
    )


def hidden_kernel(width, kept, received, dots, hidden, gain, inv_rms, grad_out, dot_out):
    quarter = kept.shape[1]
    inv = inv_rms[...]
    row_dot = (dots[...] + joined_column(received[:, quarter:])) / inv
    wide = jnp.broadcast_to(row_dot * (1.0 / math.sqrt(width)), (row_dot.shape[0], HD))
    dot_out[...] = wide.T[:1]
    scaled = gain[...] * (kept[...] + received[:, :quarter].astype(F32))
    grad_out[...] = (
        inv * scaled - hidden[...].astype(F32) * (inv * inv * inv * row_dot * (1.0 / width))
    ).astype(BF16)


def body(
    hidden,
    hidden_gain,
    neighbour_states,
    encoder_gain,
    query_weight,
    kv_weight,
    attn_grad,
    neighbour_ids,
    valid_counts,
):
    seq_size = lax.axis_size("seq")
    outer = seq_size // 2
    row_count, model_width = hidden.shape
    local_cols = query_weight.shape[1]
    cols = local_cols // 2
    slot_total, nb_length, enc_width = neighbour_states.shape
    block_len = row_count // neighbour_ids.shape[0]
    offset = block_len - 1
    piece = enc_width // (2 * seq_size)
    backward = [(i, i - 1) for i in range(1, seq_size)]

    hn, inv_rms, hidden_part, gain_part, columns_kept, columns_send = norm_columns(
        hidden, hidden_gain, outer
    )
    keep, send, pair, cross = query_part(hn, query_weight, attn_grad, block_len)
    other = swapped(send, "section", 1)
    pair_in = lax.ppermute(pair, "seq", backward)
    cross_in = lax.ppermute(
        cross,
        ("section", "seq"),
        [(s * seq_size + i, (1 - s) * seq_size + j) for s in range(2) for i, j in backward],
    )
    kv, turned = pool_project(
        neighbour_states.reshape(slot_total * nb_length, enc_width), encoder_gain, kv_weight
    )

    def attention(chunk, ahead, before):
        return attend(
            chunk, neighbour_ids, valid_counts, after(keep, ahead), other, pair_in, cross_in,
            attn_grad, kv, before,
        )

    def three_ways(pieces, mask):
        near, side, cross = pieces
        pairs = [(s * seq_size + i, (1 - s) * seq_size + (i ^ mask)) for s in range(2) for i in range(seq_size)]
        crossed = lax.ppermute(cross, ("section", "seq"), pairs)
        return swapped(near, "seq", mask), swapped(side, "section", 1), crossed

    columns_in = swapped(columns_send, "seq", outer)
    columns_mine = columns_exchange(columns_kept, columns_in, outer)
    columns_theirs = [swapped(column, "mp", 1) for column in columns_mine]

    steps = list(range(outer))
    *before, first_turned = attention(0, turned, ())
    dq, dots, dq_lead, second_turned = attention(1, turned, before)
    carried = lax.ppermute(dq_lead, "seq", [(i, i + 1) for i in range(seq_size - 1)])
    first_send, first_kept = kv_part(0, turned, after(first_turned, dq), [steps])
    first_in = swapped(first_send, "seq", 1)
    odd_send, odd_kept, even_send, even_kept = kv_part(
        1, turned, after(second_turned, first_kept), [steps[1::2], steps[::2]]
    )
    own_dq, own_grads = call(
        functools.partial(own_kernel, offset),
        "own_tokens",
        [shape((row_count, cols + HD), BF16), shape((1, row_count, cols), BF16)],
        [dq, dots, carried],
        flops=OWN_FLOPS,
    )
    odd_in = swapped(after(odd_send, own_grads), "seq", 1)
    even_in = swapped(even_send, "seq", 1)
    dq_other = swapped(own_dq, "section", 1)

    gathered = outer_gather(own_grads, outer, columns_mine[1:])

    odd_sums = both_chunks(
        odd_kernel, "odd_sums", BF16, ODD_FLOPS, first_kept, first_in, odd_kept, odd_in
    )
    kv_received = swapped(odd_sums, "seq", 2)
    kv_kept = both_chunks(
        even_kernel, "even_sums", F32, 0, first_kept, first_in, even_kept, even_in
    )
    bit = 2
    while 2 * bit < outer:
        kv_kept, kv_send = fold(kv_kept, kv_received)
        kv_received = swapped(kv_send, "seq", 2 * bit)
        bit *= 2

    weight_keep, *weight_send = weight_part(columns_mine, columns_theirs, gathered)
    weight_in = three_ways(weight_send, 1)

    normed_keep, normed_dots, normed_send = normed_part(own_dq, dq_other, query_weight)
    normed_in = swapped(normed_send, "mp", 1)
    hidden_grad, norm_dot = call(
        functools.partial(hidden_kernel, model_width),
        "hidden_grad",
        [shape(hidden_part.shape, BF16), shape((1, row_count), F32)],
        [normed_keep, normed_in, normed_dots, hidden_part, gain_part, inv_rms],
    )

    kv_mine, *kv_send = outer_sums(kv_kept, kv_received)
    kv_in = three_ways(kv_send, seq_size // 2)

    query_grad = call(
        query_grad_kernel,
        "query_grad",
        [shape((weight_keep.shape[0], local_cols), F32)],
        [weight_keep, *weight_in],
    )[0]
    kv_grad = call(
        kv_grad_kernel,
        "kv_grad",
        [shape((2, piece, local_cols), F32)],
        [after(kv_mine, query_grad), *kv_in],
    )[0]
    return (hidden_grad, query_grad, kv_grad, norm_dot.reshape(row_count))


def solution(mesh):
    placed = (
        P("seq", None),
        P(),
        P("seq", None, None),
        P(),
        P("section", "mp"),
        P(None, None, "mp"),
        P("seq", "mp"),
        P("seq", None),
        P("seq"),
    )
    return jax.shard_map(
        body,
        mesh=mesh,
        in_specs=placed,
        out_specs=(
            P("seq", ("section", "mp")),
            P(("section", "seq"), "mp"),
            P(None, ("section", "seq"), "mp"),
            P("seq"),
        ),
        check_vma=False,
    )
```

profile of v0, /device:TPU:0, one launch (start us, length us, event | category | flops | bytes accessed | tf_op | source)
XLA Modules:
  0.0 77.3 jit_solution(2003602457837331877)
XLA Ops:
  0.7 1.4 %copy-done.7 = bf16[128,4096]{1,0:T(8,128)(2,1)S(1)} copy-done((bf16[128,4096]{1,0:T(8,128)(2,1)S(1)}, bf16[128,4096]{1,0:T(8,128)(2,1)}, u32[]{:S(2)}) %copy-start.7) | copy-done | bytes 1048600
  2.0 1.0 %copy-done.8 = bf16[4096]{0:T(1024)(128)(2,1)S(1)} copy-done((bf16[4096]{0:T(1024)(128)(2,1)S(1)}, bf16[4096]{0:T(1024)(128)(2,1)}, u32[]{:S(2)}) %copy-start.8) | copy-done | bytes 8216
  3.0 0.7 norm_columns.1
  3.7 0.0 copy-start.1
  3.7 0.0 copy-start.4
  3.7 0.8 %query_part.1 = (f32[128,512]{1,0:T(8,128)S(1)}, bf16[128,512]{1,0:T(8,128)(2,1)S(1)}, bf16[2,64,512]{2,1,0:T(8,128)(2,1)S(1)}, bf16[64,512]{1,0:T(8,128)(2,1)S(1)}) custom-call(bf16[128,4096]{1,0:T(8,128)(2,1)S(1)} %get-tuple-element.52.hn, bf16[2048,1024]{1,0:T(8,128)(2,1)S(1)} %copy-done, bf16[128,1024]{1,0:T(8,128)(2,1)S(1)} %copy-done.3), custom_call_target="tpu_custom_call" | custom-call | tf_op jit(solution)/shard_map/query_part/pallas_call | solution.py:38
  4.6 3.0 %collective-permute-start = (bf16[128,512]{1,0:T(8,128)(2,1)S(1)}, bf16[128,512]{1,0:T(8,128)(2,1)S(1)}, u32[]{:S(2)}, u32[]{:S(2)}) collective-permute-start(bf16[128,512]{1,0:T(8,128)(2,1)S(1)} %get-tuple-element.56), channel_id=1, source_target_pairs={{0,16},{16,0},{1,17},{17,1},{2,18},{18,2},{3,19},{19,3},{4,20},{20... | collective-permute-start | bytes 393224 | tf_op jit(solution)/shard_map/ppermute | solution.py:56
  7.6 1.3 %collective-permute-start.1 = (bf16[2,64,512]{2,1,0:T(8,128)(2,1)S(1)}, bf16[2,64,512]{2,1,0:T(8,128)(2,1)S(1)}, u32[]{:S(2)}, u32[]{:S(2)}) collective-permute-start(bf16[2,64,512]{2,1,0:T(8,128)(2,1)S(1)} %get-tuple-element.57), channel_id=1, source_target_pairs={{2,0},{4,2},{6,4},{8,6},{10,8},{12,10},{14,12},{3,1},{5,3},{7,5},{... | collective-permute-start | bytes 393224 | tf_op jit(solution)/shard_map/ppermute | solution.py:569
  8.9 1.3 %collective-permute-start.2 = (bf16[64,512]{1,0:T(8,128)(2,1)S(1)}, bf16[64,512]{1,0:T(8,128)(2,1)S(1)}, u32[]{:S(2)}, u32[]{:S(2)}) collective-permute-start(bf16[64,512]{1,0:T(8,128)(2,1)S(1)} %get-tuple-element.58), channel_id=1, source_target_pairs={{2,16},{4,18},{6,20},{8,22},{10,24},{12,26},{14,28},{18,0},{20,2},... | collective-permute-start | bytes 196616 | tf_op jit(solution)/shard_map/ppermute | solution.py:570
  10.2 5.7 %collective-permute-start.6 = (bf16[1,2,512,128]{3,2,1,0:T(8,128)(2,1)S(1)}, bf16[1,2,512,128]{3,2,1,0:T(8,128)(2,1)S(1)}, u32[]{:S(2)}, u32[]{:S(2)}) collective-permute-start(bf16[1,2,512,128]{3,2,1,0:T(8,128)(2,1)S(1)} %get-tuple-element.74), channel_id=1, source_target_pairs={{0,8},{2,10},{4,12},{6,14},{8,0},{10,2},{12,4},{14,6},{1,9},{3,11}... | collective-permute-start | bytes 786440 | tf_op jit(solution)/shard_map/ppermute | solution.py:56
  16.0 5.3 %pool_project.1 = (bf16[2,2048,512]{2,1,0:T(8,128)(2,1)S(1)}, bf16[896,2048]{1,0:T(8,128)(2,1)S(1)}) custom-call(bf16[896]{0:T(1024)(128)(2,1)S(1)} %copy-done.4, bf16[2048,896]{1,0:T(8,128)(2,1)S(1)} %bitcast.2, bf16[2,896,1024]{2,1,0:T(8,128)(2,1)S(1)} %copy-done.2), custom_call_target="tpu_custom_call" | custom-call | tf_op jit(solution)/shard_map/pool_project/pallas_call | solution.py:38
  21.3 2.9 %attend_0.1 = (bf16[128,256]{1,0:T(8,128)(2,1)S(1)}, f32[128,1]{1,0:T(8,128)S(1)}, bf16[512,2048]{1,0:T(8,128)(2,1)S(1)}) custom-call(s32[2,16]{1,0:T(2,128)S(1)} %copy-done.5, s32[2]{0:T(128)S(1)} %copy-done.6, f32[128,512]{1,0:T(8,128)S(1)} %get-tuple-element.55.keep, bf16[128,512]{1,0:T(8,128)(2,1)S(1)} %collective-permute-done.other, ...), custom_call_target="tpu_custom_call" | custom-call | flops 4000000000 | tf_op jit(solution)/shard_map/attend_0/pallas_call | solution.py:38
  24.2 2.9 %attend_1.1 = (bf16[128,512]{1,0:T(8,128)(2,1)S(1)}, bf16[128,128]{1,0:T(8,128)(2,1)S(1)}, bf16[64,640]{1,0:T(8,128)(2,1)S(1)}, bf16[512,2048]{1,0:T(8,128)(2,1)S(1)}) custom-call(s32[2,16]{1,0:T(2,128)S(1)} %copy-done.5, s32[2]{0:T(128)S(1)} %copy-done.6, f32[128,512]{1,0:T(8,128)S(1)} %get-tuple-element.55.keep, ...), custom_call_target="tpu_custom_call" | custom-call | tf_op jit(solution)/shard_map/attend_1/pallas_call | solution.py:38
  27.1 3.6 %collective-permute-start.3 = (bf16[64,640]{1,0:T(8,128)(2,1)S(1)}, bf16[64,640]{1,0:T(8,128)(2,1)S(1)}, u32[]{:S(2)}, u32[]{:S(2)}) collective-permute-start(bf16[64,640]{1,0:T(8,128)(2,1)S(1)} %get-tuple-element.64), channel_id=1, source_target_pairs={{0,2},{2,4},{4,6},{6,8},{8,10},{10,12},{12,14},{1,3},{3,5},{5,7},{... | collective-permute-start | bytes 245768 | tf_op jit(solution)/shard_map/ppermute | solution.py:598
  30.7 2.2 %kv_part_0.1 = (bf16[4,2,56,512]{3,2,1,0:T(8,128)(2,1)S(1)}, f32[4,2,56,512]{3,2,1,0:T(8,128)S(1)}) custom-call(bf16[896,2048]{1,0:T(8,128)(2,1)S(1)} %get-tuple-element.54.turned, bf16[512,2048]{1,0:T(8,128)(2,1)S(1)} %get-tuple-element.84.turned_kv), custom_call_target="tpu_custom_call" | custom-call | tf_op jit(solution)/shard_map/kv_part_0/pallas_call | solution.py:38
  32.9 1.6 %collective-permute-start.15 = (bf16[4,2,56,512]{3,2,1,0:T(8,128)(2,1)S(1)}, bf16[4,2,56,512]{3,2,1,0:T(8,128)(2,1)S(1)}, u32[]{:S(2)}, u32[]{:S(2)}) collective-permute-start(bf16[4,2,56,512]{3,2,1,0:T(8,128)(2,1)S(1)} %get-tuple-element.86), channel_id=1, source_target_pairs={{0,2},{2,0},{4,6},{6,4},{8,10},{10,8},{12,14},{14,12},{1,3},{3,1},... | collective-permute-start | bytes 1376264 | tf_op jit(solution)/shard_map/ppermute | solution.py:56
  34.5 2.2 %kv_part_1.1 = (bf16[2,2,56,512]{3,2,1,0:T(8,128)(2,1)S(1)}, f32[2,2,56,512]{3,2,1,0:T(8,128)S(1)}, bf16[2,2,56,512]{3,2,1,0:T(8,128)(2,1)S(1)}, f32[2,2,56,512]{3,2,1,0:T(8,128)S(1)}) custom-call(bf16[896,2048]{1,0:T(8,128)(2,1)S(1)} %get-tuple-element.54.turned, bf16[512,2048]{1,0:T(8,128)(2,1)S(1)} %get-tuple-element.88.turned_kv), custom_call_target="tpu_custom_call" | custom-call | tf_op jit(solution)/shard_map/kv_part_1/pallas_call | solution.py:38
  36.8 3.2 %collective-permute-start.7 = (bf16[2,1,512,128]{3,2,1,0:T(8,128)(2,1)S(1)}, bf16[2,1,512,128]{3,2,1,0:T(8,128)(2,1)S(1)}, u32[]{:S(2)}, u32[]{:S(2)}) collective-permute-start(bf16[2,1,512,128]{3,2,1,0:T(8,128)(2,1)S(1)} %get-tuple-element.76), channel_id=1, source_target_pairs={{0,4},{2,6},{4,0},{6,2},{8,12},{10,14},{12,8},{14,10},{1,5},{3,7},... | collective-permute-start | bytes 786440 | tf_op jit(solution)/shard_map/ppermute | solution.py:56
  40.1 2.1 %collective-permute-start.17 = (bf16[2,2,56,512]{3,2,1,0:T(8,128)(2,1)S(1)}, bf16[2,2,56,512]{3,2,1,0:T(8,128)(2,1)S(1)}, u32[]{:S(2)}, u32[]{:S(2)}) collective-permute-start(bf16[2,2,56,512]{3,2,1,0:T(8,128)(2,1)S(1)} %get-tuple-element.93), channel_id=1, source_target_pairs={{0,2},{2,0},{4,6},{6,4},{8,10},{10,8},{12,14},{14,12},{1,3},{3,1},... | collective-permute-start | bytes 688136 | tf_op jit(solution)/shard_map/ppermute | solution.py:56
  42.1 0.5 collective-permute-start.4
  42.6 2.3 %collective-permute-done.7.refs_1_ = bf16[2,1,512,128]{3,2,1,0:T(8,128)(2,1)S(1)} collective-permute-done((bf16[2,1,512,128]{3,2,1,0:T(8,128)(2,1)S(1)}, bf16[2,1,512,128]{3,2,1,0:T(8,128)(2,1)S(1)}, u32[]{:S(2)}, u32[]{:S(2)}) %collective-permute-start.7) | collective-permute-done | bytes 262176 | tf_op jit(solution)/shard_map/ppermute | solution.py:56
  44.9 4.0 %collective-permute-done.10.refs_1_.refs_5_ = bf16[1,128,512]{2,1,0:T(8,128)(2,1)S(1)} collective-permute-done((bf16[1,128,512]{2,1,0:T(8,128)(2,1)S(1)}, bf16[1,128,512]{2,1,0:T(8,128)(2,1)S(1)}, u32[]{:S(2)}, u32[]{:S(2)}) %collective-permute-start.10) | collective-permute-done | bytes 131104 | tf_op jit(solution)/shard_map/ppermute | solution.py:56
  49.0 0.1 collective-permute-start.11
  49.1 0.1 collective-permute-start.9
  49.2 0.1 odd_sums.1
  49.2 2.0 %collective-permute-start.18 = (bf16[2,2,2,56,512]{4,3,2,1,0:T(8,128)(2,1)S(1)}, bf16[2,2,2,56,512]{4,3,2,1,0:T(8,128)(2,1)S(1)}, u32[]{:S(2)}, u32[]{:S(2)}) collective-permute-start(bf16[2,2,2,56,512]{4,3,2,1,0:T(8,128)(2,1)S(1)} %odd_sums.1), channel_id=1, source_target_pairs={{0,4},{2,6},{4,0},{6,2},{8,12},{10,14},{12,8},{14,10},{1,5},{3,7},... | collective-permute-start | bytes 1376264 | tf_op jit(solution)/shard_map/ppermute | solution.py:56
  51.2 0.5 collective-permute-start.16
  51.8 1.6 %normed_part.1 = (f32[128,1024]{1,0:T(8,128)S(1)}, f32[128,1]{1,0:T(8,128)S(1)}, bf16[128,1152]{1,0:T(8,128)(2,1)S(1)}) custom-call(bf16[128,640]{1,0:T(8,128)(2,1)S(1)} %get-tuple-element.65.own, bf16[128,640]{1,0:T(8,128)(2,1)S(1)} %collective-permute-done.4.other, bf16[2048,1024]{1,0:T(8,128)(2,1)S(1)} %copy-done), custom_call_target="tpu_custom_call" | custom-call | tf_op jit(solution)/shard_map/normed_part/pallas_call | solution.py:38
  53.4 0.1 collective-permute-start.5
  53.4 4.8 %collective-permute-done.11.refs_6_ = bf16[2,128,512]{2,1,0:T(8,128)(2,1)S(1)} collective-permute-done((bf16[2,128,512]{2,1,0:T(8,128)(2,1)S(1)}, bf16[2,128,512]{2,1,0:T(8,128)(2,1)S(1)}, u32[]{:S(2)}, u32[]{:S(2)}) %collective-permute-start.11) | collective-permute-done | bytes 262176 | tf_op jit(solution)/shard_map/ppermute | solution.py:56
  58.2 1.2 %weight_part.1 = (f32[256,512]{1,0:T(8,128)S(1)}, bf16[256,512]{1,0:T(8,128)(2,1)S(1)}, bf16[256,512]{1,0:T(8,128)(2,1)S(1)}, bf16[256,512]{1,0:T(8,128)(2,1)S(1)}) custom-call(bf16[2,1,512,128]{3,2,1,0:T(8,128)(2,1)S(1)} %get-tuple-element.75.refs_0_, bf16[2,1,512,128]{3,2,1,0:T(8,128)(2,1)S(1)} %collective-permute-done.7.refs_1_, ...), custom_call_target="tpu_custom_call" | custom-call | tf_op jit(solution)/shard_map/weight_part/pallas_call | solution.py:38
  59.5 0.1 collective-permute-start.12
  59.5 0.1 collective-permute-start.13
  59.6 0.1 collective-permute-done.16.second_in
  59.7 3.3 %collective-permute-start.14 = (bf16[256,512]{1,0:T(8,128)(2,1)S(1)}, bf16[256,512]{1,0:T(8,128)(2,1)S(1)}, u32[]{:S(2)}, u32[]{:S(2)}) collective-permute-start(bf16[256,512]{1,0:T(8,128)(2,1)S(1)} %get-tuple-element.82), channel_id=1, source_target_pairs={{0,18},{2,16},{4,22},{6,20},{8,26},{10,24},{12,30},{14,28},{16,2},... | collective-permute-start | bytes 786440 | tf_op jit(solution)/shard_map/ppermute | solution.py:588
  63.0 0.1 even_sums.1.kept
  63.1 2.1 %collective-permute-done.18.received = bf16[2,2,2,56,512]{4,3,2,1,0:T(8,128)(2,1)S(1)} collective-permute-done((bf16[2,2,2,56,512]{4,3,2,1,0:T(8,128)(2,1)S(1)}, bf16[2,2,2,56,512]{4,3,2,1,0:T(8,128)(2,1)S(1)}, u32[]{:S(2)}, u32[]{:S(2)}) %collective-permute-start.18) | collective-permute-done | bytes 458784 | tf_op jit(solution)/shard_map/ppermute | solution.py:56
  65.2 0.1 outer_sums.1
  65.3 0.1 collective-permute-start.19
  65.4 0.5 collective-permute-start.20
  65.9 1.5 %collective-permute-done.12.paired = bf16[256,512]{1,0:T(8,128)(2,1)S(1)} collective-permute-done((bf16[256,512]{1,0:T(8,128)(2,1)S(1)}, bf16[256,512]{1,0:T(8,128)(2,1)S(1)}, u32[]{:S(2)}, u32[]{:S(2)}) %collective-permute-start.12) | collective-permute-done | bytes 262176 | tf_op jit(solution)/shard_map/ppermute | solution.py:56
  67.4 2.3 %collective-permute-start.21 = (bf16[2,56,512]{2,1,0:T(8,128)(2,1)S(1)}, bf16[2,56,512]{2,1,0:T(8,128)(2,1)S(1)}, u32[]{:S(2)}, u32[]{:S(2)}) collective-permute-start(bf16[2,56,512]{2,1,0:T(8,128)(2,1)S(1)} %get-tuple-element.98), channel_id=1, source_target_pairs={{0,24},{2,26},{4,28},{6,30},{8,16},{10,18},{12,20},{14,22},{16,8},... | collective-permute-start | bytes 344072 | tf_op jit(solution)/shard_map/ppermute | solution.py:588
  69.8 1.0 %hidden_grad.1 = (bf16[128,1024]{1,0:T(8,128)(2,1)}, f32[1,128]{1,0:T(1,128)}) custom-call(f32[128,1024]{1,0:T(8,128)S(1)} %get-tuple-element.66.kept, bf16[128,1152]{1,0:T(8,128)(2,1)S(1)} %collective-permute-done.5.received, f32[128,1]{1,0:T(8,128)S(1)} %get-tuple-element.68.dots, bf16[128,1024]{1,0:T(8,128)(2,1)S(1)} %get-tuple-element.69.hidden, ...), custom_call_target="tpu_custom_call" | custom-call | tf_op jit(solution)/shard_map/hidden_grad/pallas_call | solution.py:38
  70.8 2.1 %collective-permute-done.13.side = bf16[256,512]{1,0:T(8,128)(2,1)S(1)} collective-permute-done((bf16[256,512]{1,0:T(8,128)(2,1)S(1)}, bf16[256,512]{1,0:T(8,128)(2,1)S(1)}, u32[]{:S(2)}, u32[]{:S(2)}) %collective-permute-start.13) | collective-permute-done | bytes 262176 | tf_op jit(solution)/shard_map/ppermute | solution.py:56
  72.9 1.1 %query_grad.1 = f32[256,1024]{1,0:T(8,128)} custom-call(f32[256,512]{1,0:T(8,128)S(1)} %get-tuple-element.79.kept, bf16[256,512]{1,0:T(8,128)(2,1)S(1)} %collective-permute-done.12.paired, bf16[256,512]{1,0:T(8,128)(2,1)S(1)} %collective-permute-done.13.side, bf16[256,512]{1,0:T(8,128)(2,1)S(1)} %collective-permute-done.14.cross), custom_call_target="tpu_custom_call" | custom-call | tf_op jit(solution)/shard_map/query_grad/pallas_call | solution.py:38
  74.0 0.8 %collective-permute-done.19.following = bf16[2,56,512]{2,1,0:T(8,128)(2,1)S(1)} collective-permute-done((bf16[2,56,512]{2,1,0:T(8,128)(2,1)S(1)}, bf16[2,56,512]{2,1,0:T(8,128)(2,1)S(1)}, u32[]{:S(2)}, u32[]{:S(2)}) %collective-permute-start.19) | collective-permute-done | bytes 114720 | tf_op jit(solution)/shard_map/ppermute | solution.py:56
  74.8 1.7 %collective-permute-done.21.cross = bf16[2,56,512]{2,1,0:T(8,128)(2,1)S(1)} collective-permute-done((bf16[2,56,512]{2,1,0:T(8,128)(2,1)S(1)}, bf16[2,56,512]{2,1,0:T(8,128)(2,1)S(1)}, u32[]{:S(2)}, u32[]{:S(2)}) %collective-permute-start.21) | collective-permute-done | bytes 114720 | tf_op jit(solution)/shard_map/ppermute | solution.py:588
  76.5 0.8 %kv_grad.1 = f32[2,56,1024]{2,1,0:T(8,128)} custom-call(f32[2,56,512]{2,1,0:T(8,128)S(1)} %get-tuple-element.95.mine, bf16[2,56,512]{2,1,0:T(8,128)(2,1)S(1)} %collective-permute-done.19.following, bf16[2,56,512]{2,1,0:T(8,128)(2,1)S(1)} %collective-permute-done.20.side, bf16[2,56,512]{2,1,0:T(8,128)(2,1)S(1)} %collective-permute-done.21.cross), custom_call_target="tpu_custom_call" | custom-call | tf_op jit(solution)/shard_map/kv_grad/pallas_call | solution.py:38
  (32 shorter events, 0.2 us)
Async XLA Ops:
  0.6 3.1 %copy-start = (bf16[2048,1024]{1,0:T(8,128)(2,1)S(1)}, bf16[2048,1024]{1,0:T(8,128)(2,1)}, u32[]{:S(2)}) copy-start(bf16[2048,1024]{1,0:T(8,128)(2,1)} %weight.5) | copy-start | bytes 12582916
  0.6 3.1 %copy-start.3 = (bf16[128,1024]{1,0:T(8,128)(2,1)S(1)}, bf16[128,1024]{1,0:T(8,128)(2,1)}, u32[]{:S(2)}) copy-start(bf16[128,1024]{1,0:T(8,128)(2,1)} %grad_own.3) | copy-start | bytes 786436
  0.7 1.4 %copy-start.7 = (bf16[128,4096]{1,0:T(8,128)(2,1)S(1)}, bf16[128,4096]{1,0:T(8,128)(2,1)}, u32[]{:S(2)}) copy-start(bf16[128,4096]{1,0:T(8,128)(2,1)} %hidden.1) | copy-start | bytes 3145732
  2.0 1.0 %copy-start.8 = (bf16[4096]{0:T(1024)(128)(2,1)S(1)}, bf16[4096]{0:T(1024)(128)(2,1)}, u32[]{:S(2)}) copy-start(bf16[4096]{0:T(1024)(128)(2,1)} %gain.2) | copy-start | bytes 24580
  3.0 12.9 %copy-start.2 = (bf16[2,896,1024]{2,1,0:T(8,128)(2,1)S(1)}, bf16[2,896,1024]{2,1,0:T(8,128)(2,1)}, u32[]{:S(2)}) copy-start(bf16[2,896,1024]{2,1,0:T(8,128)(2,1)} %weight.4) | copy-start | bytes 11010052
  3.7 12.2 %copy-start.1 = (bf16[16,128,896]{2,1,0:T(8,128)(2,1)S(1)}, bf16[16,128,896]{2,1,0:T(8,128)(2,1)}, u32[]{:S(2)}) copy-start(bf16[16,128,896]{2,1,0:T(8,128)(2,1)} %param.11) | copy-start | bytes 11010052
  3.7 12.2 %copy-start.4 = (bf16[896]{0:T(1024)(128)(2,1)S(1)}, bf16[896]{0:T(1024)(128)(2,1)}, u32[]{:S(2)}) copy-start(bf16[896]{0:T(1024)(128)(2,1)} %gain.3) | copy-start | bytes 5380
  4.6 16.7 %collective-permute-start = (bf16[128,512]{1,0:T(8,128)(2,1)S(1)}, bf16[128,512]{1,0:T(8,128)(2,1)S(1)}, u32[]{:S(2)}, u32[]{:S(2)}) collective-permute-start(bf16[128,512]{1,0:T(8,128)(2,1)S(1)} %get-tuple-element.56), channel_id=1, source_target_pairs={{0,16},{16,0},{1,17},{17,1},{2,18},{18,2},{3,19},{19,3},{4,20},{20... | collective-permute-start | bytes 393224 | tf_op jit(solution)/shard_map/ppermute | solution.py:56
  7.6 13.7 %collective-permute-start.1 = (bf16[2,64,512]{2,1,0:T(8,128)(2,1)S(1)}, bf16[2,64,512]{2,1,0:T(8,128)(2,1)S(1)}, u32[]{:S(2)}, u32[]{:S(2)}) collective-permute-start(bf16[2,64,512]{2,1,0:T(8,128)(2,1)S(1)} %get-tuple-element.57), channel_id=1, source_target_pairs={{2,0},{4,2},{6,4},{8,6},{10,8},{12,10},{14,12},{3,1},{5,3},{7,5},{... | collective-permute-start | bytes 393224 | tf_op jit(solution)/shard_map/ppermute | solution.py:569
  8.9 12.4 %collective-permute-start.2 = (bf16[64,512]{1,0:T(8,128)(2,1)S(1)}, bf16[64,512]{1,0:T(8,128)(2,1)S(1)}, u32[]{:S(2)}, u32[]{:S(2)}) collective-permute-start(bf16[64,512]{1,0:T(8,128)(2,1)S(1)} %get-tuple-element.58), channel_id=1, source_target_pairs={{2,16},{4,18},{6,20},{8,22},{10,24},{12,26},{14,28},{18,0},{20,2},... | collective-permute-start | bytes 196616 | tf_op jit(solution)/shard_map/ppermute | solution.py:570
  10.2 26.6 %collective-permute-start.6 = (bf16[1,2,512,128]{3,2,1,0:T(8,128)(2,1)S(1)}, bf16[1,2,512,128]{3,2,1,0:T(8,128)(2,1)S(1)}, u32[]{:S(2)}, u32[]{:S(2)}) collective-permute-start(bf16[1,2,512,128]{3,2,1,0:T(8,128)(2,1)S(1)} %get-tuple-element.74), channel_id=1, source_target_pairs={{0,8},{2,10},{4,12},{6,14},{8,0},{10,2},{12,4},{14,6},{1,9},{3,11}... | collective-permute-start | bytes 786440 | tf_op jit(solution)/shard_map/ppermute | solution.py:56
  15.9 5.3 %copy-start.5 = (s32[2,16]{1,0:T(2,128)S(1)}, s32[2,16]{1,0:T(2,128)}, u32[]{:S(2)}) copy-start(s32[2,16]{1,0:T(2,128)} %ids.3) | copy-start | bytes 388
  15.9 5.3 %copy-start.6 = (s32[2]{0:T(128)S(1)}, s32[2]{0:T(128)}, u32[]{:S(2)}) copy-start(s32[2]{0:T(128)} %counts.3) | copy-start | bytes 28
  27.1 13.0 %collective-permute-start.3 = (bf16[64,640]{1,0:T(8,128)(2,1)S(1)}, bf16[64,640]{1,0:T(8,128)(2,1)S(1)}, u32[]{:S(2)}, u32[]{:S(2)}) collective-permute-start(bf16[64,640]{1,0:T(8,128)(2,1)S(1)} %get-tuple-element.64), channel_id=1, source_target_pairs={{0,2},{2,4},{4,6},{6,8},{8,10},{10,12},{12,14},{1,3},{3,5},{5,7},{... | collective-permute-start | bytes 245768 | tf_op jit(solution)/shard_map/ppermute | solution.py:598
  32.9 16.3 %collective-permute-start.15 = (bf16[4,2,56,512]{3,2,1,0:T(8,128)(2,1)S(1)}, bf16[4,2,56,512]{3,2,1,0:T(8,128)(2,1)S(1)}, u32[]{:S(2)}, u32[]{:S(2)}) collective-permute-start(bf16[4,2,56,512]{3,2,1,0:T(8,128)(2,1)S(1)} %get-tuple-element.86), channel_id=1, source_target_pairs={{0,2},{2,0},{4,6},{6,4},{8,10},{10,8},{12,14},{14,12},{1,3},{3,1},... | collective-permute-start | bytes 1376264 | tf_op jit(solution)/shard_map/ppermute | solution.py:56
  36.8 8.1 %collective-permute-start.7 = (bf16[2,1,512,128]{3,2,1,0:T(8,128)(2,1)S(1)}, bf16[2,1,512,128]{3,2,1,0:T(8,128)(2,1)S(1)}, u32[]{:S(2)}, u32[]{:S(2)}) collective-permute-start(bf16[2,1,512,128]{3,2,1,0:T(8,128)(2,1)S(1)} %get-tuple-element.76), channel_id=1, source_target_pairs={{0,4},{2,6},{4,0},{6,2},{8,12},{10,14},{12,8},{14,10},{1,5},{3,7},... | collective-permute-start | bytes 786440 | tf_op jit(solution)/shard_map/ppermute | solution.py:56
  40.1 9.0 %collective-permute-start.17 = (bf16[2,2,56,512]{3,2,1,0:T(8,128)(2,1)S(1)}, bf16[2,2,56,512]{3,2,1,0:T(8,128)(2,1)S(1)}, u32[]{:S(2)}, u32[]{:S(2)}) collective-permute-start(bf16[2,2,56,512]{3,2,1,0:T(8,128)(2,1)S(1)} %get-tuple-element.93), channel_id=1, source_target_pairs={{0,2},{2,0},{4,6},{6,4},{8,10},{10,8},{12,14},{14,12},{1,3},{3,1},... | collective-permute-start | bytes 688136 | tf_op jit(solution)/shard_map/ppermute | solution.py:56
  42.1 6.8 %collective-permute-start.10 = (bf16[1,128,512]{2,1,0:T(8,128)(2,1)S(1)}, bf16[1,128,512]{2,1,0:T(8,128)(2,1)S(1)}, u32[]{:S(2)}, u32[]{:S(2)}) collective-permute-start(bf16[1,128,512]{2,1,0:T(8,128)(2,1)S(1)} %get-tuple-element.78.refs_0_.refs_4_), channel_id=1, source_target_pairs={{0,8},{2,10},{4,12},{6,14},{8,0},{10,2},{12,4},{14,6},{1,9},{3,11}... | collective-permute-start | bytes 393224 | tf_op jit(solution)/shard_map/ppermute | solution.py:56
  42.1 9.1 %collective-permute-start.4 = (bf16[128,640]{1,0:T(8,128)(2,1)S(1)}, bf16[128,640]{1,0:T(8,128)(2,1)S(1)}, u32[]{:S(2)}, u32[]{:S(2)}) collective-permute-start(bf16[128,640]{1,0:T(8,128)(2,1)S(1)} %get-tuple-element.65.own), channel_id=1, source_target_pairs={{0,16},{16,0},{1,17},{17,1},{2,18},{18,2},{3,19},{19,3},{4,20},{20... | collective-permute-start | bytes 491528 | tf_op jit(solution)/shard_map/ppermute | solution.py:56
  44.9 8.5 %collective-permute-start.8 = (bf16[2,1,512,128]{3,2,1,0:T(8,128)(2,1)S(1)}, bf16[2,1,512,128]{3,2,1,0:T(8,128)(2,1)S(1)}, u32[]{:S(2)}, u32[]{:S(2)}) collective-permute-start(bf16[2,1,512,128]{3,2,1,0:T(8,128)(2,1)S(1)} %get-tuple-element.75.refs_0_), channel_id=1, source_target_pairs={{0,1},{1,0},{2,3},{3,2},{4,5},{5,4},{6,7},{7,6},{8,9},{9,8},{10,11... | collective-permute-start | bytes 786440 | tf_op jit(solution)/shard_map/ppermute | solution.py:56
  49.0 9.2 %collective-permute-start.11 = (bf16[2,128,512]{2,1,0:T(8,128)(2,1)S(1)}, bf16[2,128,512]{2,1,0:T(8,128)(2,1)S(1)}, u32[]{:S(2)}, u32[]{:S(2)}) collective-permute-start(bf16[2,128,512]{2,1,0:T(8,128)(2,1)S(1)} %stacked.1), channel_id=1, source_target_pairs={{0,4},{2,6},{4,0},{6,2},{8,12},{10,14},{12,8},{14,10},{1,5},{3,7},... | collective-permute-start | bytes 786440 | tf_op jit(solution)/shard_map/ppermute | solution.py:56
  49.1 9.2 %collective-permute-start.9 = (bf16[2,1,512,128]{3,2,1,0:T(8,128)(2,1)S(1)}, bf16[2,1,512,128]{3,2,1,0:T(8,128)(2,1)S(1)}, u32[]{:S(2)}, u32[]{:S(2)}) collective-permute-start(bf16[2,1,512,128]{3,2,1,0:T(8,128)(2,1)S(1)} %collective-permute-done.7.refs_1_), channel_id=1, source_target_pairs={{0,1},{1,0},{2,3},{3,2},{4,5},{5,4},{6,7},{7,6},{8,9},{9,8},{10,11... | collective-permute-start | bytes 786440 | tf_op jit(solution)/shard_map/ppermute | solution.py:56
  49.2 16.0 %collective-permute-start.18 = (bf16[2,2,2,56,512]{4,3,2,1,0:T(8,128)(2,1)S(1)}, bf16[2,2,2,56,512]{4,3,2,1,0:T(8,128)(2,1)S(1)}, u32[]{:S(2)}, u32[]{:S(2)}) collective-permute-start(bf16[2,2,2,56,512]{4,3,2,1,0:T(8,128)(2,1)S(1)} %odd_sums.1), channel_id=1, source_target_pairs={{0,4},{2,6},{4,0},{6,2},{8,12},{10,14},{12,8},{14,10},{1,5},{3,7},... | collective-permute-start | bytes 1376264 | tf_op jit(solution)/shard_map/ppermute | solution.py:56
  51.2 8.4 %collective-permute-start.16 = (bf16[2,2,56,512]{3,2,1,0:T(8,128)(2,1)S(1)}, bf16[2,2,56,512]{3,2,1,0:T(8,128)(2,1)S(1)}, u32[]{:S(2)}, u32[]{:S(2)}) collective-permute-start(bf16[2,2,56,512]{3,2,1,0:T(8,128)(2,1)S(1)} %get-tuple-element.90), channel_id=1, source_target_pairs={{0,2},{2,0},{4,6},{6,4},{8,10},{10,8},{12,14},{14,12},{1,3},{3,1},... | collective-permute-start | bytes 688136 | tf_op jit(solution)/shard_map/ppermute | solution.py:56
  53.4 12.0 %collective-permute-start.5 = (bf16[128,1152]{1,0:T(8,128)(2,1)S(1)}, bf16[128,1152]{1,0:T(8,128)(2,1)S(1)}, u32[]{:S(2)}, u32[]{:S(2)}) collective-permute-start(bf16[128,1152]{1,0:T(8,128)(2,1)S(1)} %get-tuple-element.67), channel_id=1, source_target_pairs={{0,1},{1,0},{2,3},{3,2},{4,5},{5,4},{6,7},{7,6},{8,9},{9,8},{10,11... | collective-permute-start | bytes 884744 | tf_op jit(solution)/shard_map/ppermute | solution.py:56
  59.5 8.0 %collective-permute-start.12 = (bf16[256,512]{1,0:T(8,128)(2,1)S(1)}, bf16[256,512]{1,0:T(8,128)(2,1)S(1)}, u32[]{:S(2)}, u32[]{:S(2)}) collective-permute-start(bf16[256,512]{1,0:T(8,128)(2,1)S(1)} %get-tuple-element.80), channel_id=1, source_target_pairs={{0,2},{2,0},{4,6},{6,4},{8,10},{10,8},{12,14},{14,12},{1,3},{3,1},... | collective-permute-start | bytes 786440 | tf_op jit(solution)/shard_map/ppermute | solution.py:56
  59.5 13.3 %collective-permute-start.13 = (bf16[256,512]{1,0:T(8,128)(2,1)S(1)}, bf16[256,512]{1,0:T(8,128)(2,1)S(1)}, u32[]{:S(2)}, u32[]{:S(2)}) collective-permute-start(bf16[256,512]{1,0:T(8,128)(2,1)S(1)} %get-tuple-element.81), channel_id=1, source_target_pairs={{0,16},{16,0},{1,17},{17,1},{2,18},{18,2},{3,19},{19,3},{4,20},{20... | collective-permute-start | bytes 786440 | tf_op jit(solution)/shard_map/ppermute | solution.py:56
  59.7 13.2 %collective-permute-start.14 = (bf16[256,512]{1,0:T(8,128)(2,1)S(1)}, bf16[256,512]{1,0:T(8,128)(2,1)S(1)}, u32[]{:S(2)}, u32[]{:S(2)}) collective-permute-start(bf16[256,512]{1,0:T(8,128)(2,1)S(1)} %get-tuple-element.82), channel_id=1, source_target_pairs={{0,18},{2,16},{4,22},{6,20},{8,26},{10,24},{12,30},{14,28},{16,2},... | collective-permute-start | bytes 786440 | tf_op jit(solution)/shard_map/ppermute | solution.py:588
  65.3 9.5 %collective-permute-start.19 = (bf16[2,56,512]{2,1,0:T(8,128)(2,1)S(1)}, bf16[2,56,512]{2,1,0:T(8,128)(2,1)S(1)}, u32[]{:S(2)}, u32[]{:S(2)}) collective-permute-start(bf16[2,56,512]{2,1,0:T(8,128)(2,1)S(1)} %get-tuple-element.96), channel_id=1, source_target_pairs={{0,8},{2,10},{4,12},{6,14},{8,0},{10,2},{12,4},{14,6},{1,9},{3,11}... | collective-permute-start | bytes 344072 | tf_op jit(solution)/shard_map/ppermute | solution.py:56
  65.4 9.4 %collective-permute-start.20 = (bf16[2,56,512]{2,1,0:T(8,128)(2,1)S(1)}, bf16[2,56,512]{2,1,0:T(8,128)(2,1)S(1)}, u32[]{:S(2)}, u32[]{:S(2)}) collective-permute-start(bf16[2,56,512]{2,1,0:T(8,128)(2,1)S(1)} %get-tuple-element.97), channel_id=1, source_target_pairs={{0,16},{16,0},{1,17},{17,1},{2,18},{18,2},{3,19},{19,3},{4,20},{20... | collective-permute-start | bytes 344072 | tf_op jit(solution)/shard_map/ppermute | solution.py:56
  67.4 9.1 %collective-permute-start.21 = (bf16[2,56,512]{2,1,0:T(8,128)(2,1)S(1)}, bf16[2,56,512]{2,1,0:T(8,128)(2,1)S(1)}, u32[]{:S(2)}, u32[]{:S(2)}) collective-permute-start(bf16[2,56,512]{2,1,0:T(8,128)(2,1)S(1)} %get-tuple-element.98), channel_id=1, source_target_pairs={{0,24},{2,26},{4,28},{6,30},{8,16},{10,18},{12,20},{14,22},{16,8},... | collective-permute-start | bytes 344072 | tf_op jit(solution)/shard_map/ppermute | solution.py:588
where the time goes:
time: 77.6 us; the launch traced here: 77.3 us
  starting transfers between devices  31.5 us (41%)
  Pallas kernels  23 us (30%)
  waiting for transfers between devices  19.5 us (25%)
  local copies, waits for them, and re-layouts  2.36 us (3%)
  between operations  0.96 us (1%)
    pallas_call x18, Pallas kernels, call(): pl.pallas_call(kernel, in_specs=in_specs or [IN_VMEM] * len(operands), ou...  23 us
    ppermute x17, starting transfers between devices, swapped(): return lax.ppermute(array, axis, [(i, i ^ mask) for i in range(size)])  19.6 us
    ppermute x17, waiting for transfers between devices, swapped(): return lax.ppermute(array, axis, [(i, i ^ mask) for i in range(size)])  17.8 us
    ppermute x2, starting transfers between devices, three_ways(): crossed = lax.ppermute(cross, ('section', 'seq'), pairs)  5.68 us
    ppermute x1, starting transfers between devices, body(): lax.ppermute(dq_lead, 'seq', [(i, i + 1) for i in range(seq_size - 1)])  3.58 us
    unnamed x18, local copies, waits for them, and re-layouts  2.36 us
    ppermute x2, waiting for transfers between devices, three_ways(): crossed = lax.ppermute(cross, ('section', 'seq'), pairs)  1.73 us
  transfers between devices with their start and end apart: 22, of which 9 were waited for; matrix products, arithmetic and copies ran while one was open for 0% of the time, Pallas kernels for 27%

commit v1 on v0

--- a/solution.py
+++ b/solution.py
@@ -15,7 +15,7 @@
 VMEM_BYTES = 24 * 1024 * 1024
 CHUNKS = 2
 NORM_FLOPS = 3_000_000_000
-FIRST_ATTEND_FLOPS = 4_000_000_000
+ATTEND_FLOPS = 4_000_000_000
 OUTER_FLOPS = 80_000_000
 OWN_FLOPS = 2_000_000_000
 ODD_FLOPS = 1_000_000_000
@@ -218,20 +218,11 @@
 
 
 def attend_kernel(
-    chunk, slot_count, ids, counts, keep, other, pair, cross, grad_own, kv, *rest
+    slot_count, ids, counts, keep, other, pair, cross, grad_own, kv, dq_out, dots_out, lead_out, *rest
 ):
-    last = chunk == CHUNKS - 1
-    if chunk > 0:
-        before, dots_before, *rest = rest
-    dq_out, dots_out, *rest = rest
-    if last:
-        lead_out, *rest = rest
-    turned_kv, bias = rest
+    *turned_kv, bias = rest
     section = lax.axis_index("section")
-    rows, all_cols = keep.shape
-    cols = all_cols // CHUNKS
-    left = chunk * cols
-    here = slice(left, left + cols)
+    rows, cols = keep.shape
     lead = cross.shape[0]
     keys = kv.shape[1]
     block_count = counts.shape[0]
@@ -249,23 +240,20 @@
             line, (block_len, keys)
         )
     following = lax.broadcasted_iota(jnp.int32, (rows, 1), 0) < offset
-    own = keep[:, here] + other[:, here].astype(F32)
-    led = pair[0, :, here].astype(F32) + cross[:, here].astype(F32)
+    own = keep[...] + other[...].astype(F32)
+    led = pair[0].astype(F32) + cross[...].astype(F32)
     padding = jnp.zeros((rows - lead, cols), F32)
     queries = jnp.where(following, jnp.concatenate([led, padding], 0), own)
-    own = lanes_at(grad_own, section * all_cols + left, cols).astype(F32)
-    led = pair[1, :, here].astype(F32)
-    grads = jnp.where(following, jnp.concatenate([led, padding], 0), own)
+    own = lanes_at(grad_own, section * cols, cols).astype(F32)
+    grads = jnp.where(following, jnp.concatenate([pair[1].astype(F32), padding], 0), own)
     rolled_queries = pltpu.roll(queries, rows - offset, 0)
     rolled_grads = pltpu.roll(grads, rows - offset, 0)
-    dots = dots_before[...] if chunk > 0 else jnp.zeros((rows, 1), F32)
-    if chunk > 0:
-        dq_out[:, :left] = before[...]
+    dots = jnp.zeros((rows, 1), F32)
+    span = cols // CHUNKS
     for head in range(cols // HD):
-        span = slice(head * HD, (head + 1) * HD)
-        at = slice(left + head * HD, left + (head + 1) * HD)
-        query = rolled_queries[:, span].astype(BF16)
-        grad = rolled_grads[:, span].astype(BF16)
+        at = slice(head * HD, (head + 1) * HD)
+        query = rolled_queries[:, at].astype(BF16)
+        grad = rolled_grads[:, at].astype(BF16)
         key = kv[0, :, at]
         value = kv[1, :, at]
         scores = nt_dot(query, key) * (factor * LOG2_E) + bias[...]
@@ -278,22 +266,21 @@
         scale = norm * factor
         dq = jnp.dot(grad_scores, key, preferred_element_type=F32) * scale
         dq = pltpu.roll(dq, offset, 0).astype(BF16)
-        dots = dots + jnp.sum(dq.astype(F32) * queries[:, span], axis=1, keepdims=True)
+        dots = dots + jnp.sum(dq.astype(F32) * queries[:, at], axis=1, keepdims=True)
         dq_out[:, at] = dq
         turned_query = (query.astype(F32) * scale).T.astype(BF16)
-        turned_grad = (rolled_grads[:, span] * norm).T.astype(BF16)
-        turned_kv[span, :] = jnp.dot(
+        turned_grad = (rolled_grads[:, at] * norm).T.astype(BF16)
+        out = turned_kv[head * HD // span]
+        base = head * HD % span
+        out[base : base + HD, :] = jnp.dot(
             turned_query, grad_scores, preferred_element_type=F32
         ).astype(BF16)
-        turned_kv[cols + head * HD : cols + (head + 1) * HD, :] = jnp.dot(
+        out[span + base : span + base + HD, :] = jnp.dot(
             turned_grad, weights.astype(BF16), preferred_element_type=F32
         ).astype(BF16)
-    if last:
-        dots_out[...] = split_column(dots)
-        lead_out[:, :all_cols] = dq_out[:lead]
-        lead_out[:, all_cols:] = dots_out[:lead]
-    else:
-        dots_out[...] = dots
+    dots_out[...] = split_column(dots)
+    lead_out[:, :cols] = dq_out[:lead]
+    lead_out[:, cols:] = dots_out[:lead]
 
 
 def kv_part_kernel(groups, turned, turned_kv, *rest):
@@ -311,28 +298,24 @@
                     out[index, part] = rows_at(product, start, piece).astype(out.dtype)
 
 
-def attend(chunk, ids, counts, keep, other, pair, cross, attn_grad, kv, before):
-    rows, all_cols = keep.shape
-    cols = all_cols // CHUNKS
+def attend(ids, counts, keep, other, pair, cross, attn_grad, kv):
+    rows, cols = keep.shape
     lead = cross.shape[0]
     keys = kv.shape[1]
-    last = chunk == CHUNKS - 1
-    operands = [ids, counts, keep, other, pair, cross, attn_grad, kv, *before]
-    out_shape = [
-        shape((rows, (chunk + 1) * cols), BF16),
-        shape((rows, HD), BF16) if last else shape((rows, 1), F32),
-    ]
-    if last:
-        out_shape.append(shape((lead, all_cols + HD), BF16))
-    out_shape.append(shape((2 * cols, keys), BF16))
-    return call(
-        functools.partial(attend_kernel, chunk, ids.shape[1]),
-        "attend_%d" % chunk,
-        out_shape,
+    operands = [ids, counts, keep, other, pair, cross, attn_grad, kv]
+    return call(
+        functools.partial(attend_kernel, ids.shape[1]),
+        "attend",
+        [
+            shape((rows, cols), BF16),
+            shape((rows, HD), BF16),
+            shape((lead, cols + HD), BF16),
+            *[shape((2 * cols // CHUNKS, keys), BF16)] * CHUNKS,
+        ],
         operands,
         [IN_SMEM] * 2 + [IN_VMEM] * (len(operands) - 2),
         [pltpu.VMEM((rows, keys), F32)],
-        0 if last else FIRST_ATTEND_FLOPS,
+        ATTEND_FLOPS,
     )
 
 
@@ -415,7 +398,7 @@
     )
 
 
-def kv_grad_kernel(mine, following, side, cross, out):
+def kv_grad_kernel(mine, following, cross, side, out):
     section = lax.axis_index("section")
     cols = mine.shape[2] // 2
     for chunk in range(CHUNKS):
@@ -489,7 +472,7 @@
     return stages
 
 
-def query_grad_kernel(kept, paired, side, cross, out):
+def query_grad_kernel(kept, paired, cross, side, out):
     section = lax.axis_index("section")
     cols = kept.shape[1]
     own = pl.ds(pl.multiple_of(section * cols, cols), cols)
@@ -576,37 +559,35 @@
         neighbour_states.reshape(slot_total * nb_length, enc_width), encoder_gain, kv_weight
     )
 
-    def attention(chunk, ahead, before):
-        return attend(
-            chunk, neighbour_ids, valid_counts, after(keep, ahead), other, pair_in, cross_in,
-            attn_grad, kv, before,
-        )
-
     def three_ways(pieces, mask):
         near, side, cross = pieces
         pairs = [(s * seq_size + i, (1 - s) * seq_size + (i ^ mask)) for s in range(2) for i in range(seq_size)]
-        crossed = lax.ppermute(cross, ("section", "seq"), pairs)
-        return swapped(near, "seq", mask), swapped(side, "section", 1), crossed
+        return (
+            swapped(near, "seq", mask),
+            lax.ppermute(cross, ("section", "seq"), pairs),
+            swapped(side, "section", 1),
+        )
 
     columns_in = swapped(columns_send, "seq", outer)
     columns_mine = columns_exchange(columns_kept, columns_in, outer)
     columns_theirs = [swapped(column, "mp", 1) for column in columns_mine]
 
     steps = list(range(outer))
-    *before, first_turned = attention(0, turned, ())
-    dq, dots, dq_lead, second_turned = attention(1, turned, before)
+    dq, dots, dq_lead, first_turned, second_turned = attend(
+        neighbour_ids, valid_counts, after(keep, turned), other, pair_in, cross_in, attn_grad, kv
+    )
     carried = lax.ppermute(dq_lead, "seq", [(i, i + 1) for i in range(seq_size - 1)])
     first_send, first_kept = kv_part(0, turned, after(first_turned, dq), [steps])
     first_in = swapped(first_send, "seq", 1)
-    odd_send, odd_kept, even_send, even_kept = kv_part(
-        1, turned, after(second_turned, first_kept), [steps[1::2], steps[::2]]
-    )
     own_dq, own_grads = call(
         functools.partial(own_kernel, offset),
         "own_tokens",
         [shape((row_count, cols + HD), BF16), shape((1, row_count, cols), BF16)],
         [dq, dots, carried],
         flops=OWN_FLOPS,
+    )
+    odd_send, odd_kept, even_send, even_kept = kv_part(
+        1, turned, after(second_turned, first_kept), [steps[1::2], steps[::2]]
     )
     odd_in = swapped(after(odd_send, own_grads), "seq", 1)
     even_in = swapped(even_send, "seq", 1)

time: 77.6 us -> 77.2 us (level)
  starting transfers between devices: 31.5 us -> 33.1 us
  waiting for transfers between devices: 19.5 us -> 18.5 us
  Pallas kernels: 23 us -> 22.1 us
    ppermute x17, starting transfers between devices: 19.6 us -> 23 us  [swapped(): return lax.ppermute(array, axis, [(i, i ^ mask) for i in range(size)])]
    ppermute x2, starting transfers between devices: 5.68 us -> 3.93 us  [three_ways(): lax.ppermute(cross, ('section', 'seq'), pairs)]
    ppermute x17, waiting for transfers between devices: 17.8 us -> 16.8 us  [swapped(): return lax.ppermute(array, axis, [(i, i ^ mask) for i in range(size)])]
    pallas_call x18 -> x17, Pallas kernels: 23 us -> 22.1 us  [call(): pl.pallas_call(kernel, in_specs=in_specs or [IN_VMEM] * len(operands), ou...]
  transfers between devices with their start and end apart: 22 -> 22, of which waited for: 9 -> 8; matrix products, arithmetic and copies ran while one was open for 0% -> 0% of each run, Pallas kernels for 27% -> 26%
where the time goes in v1:
time: 77.2 us; the launch traced here: 77 us
  starting transfers between devices  33.1 us (43%)
  Pallas kernels  22.1 us (29%)
  waiting for transfers between devices  18.5 us (24%)
  local copies, waits for them, and re-layouts  2.36 us (3%)
  between operations  0.95 us (1%)
    ppermute x17, starting transfers between devices, swapped(): return lax.ppermute(array, axis, [(i, i ^ mask) for i in range(size)])  23 us
    pallas_call x17, Pallas kernels, call(): pl.pallas_call(kernel, in_specs=in_specs or [IN_VMEM] * len(operands), ou...  22.1 us
    ppermute x17, waiting for transfers between devices, swapped(): return lax.ppermute(array, axis, [(i, i ^ mask) for i in range(size)])  16.8 us
    ppermute x2, starting transfers between devices, three_ways(): lax.ppermute(cross, ('section', 'seq'), pairs)  3.93 us
    ppermute x1, starting transfers between devices, body(): lax.ppermute(dq_lead, 'seq', [(i, i + 1) for i in range(seq_size - 1)])  3.59 us
    unnamed x18, local copies, waits for them, and re-layouts  2.36 us
    ppermute x2, waiting for transfers between devices, three_ways(): lax.ppermute(cross, ('section', 'seq'), pairs)  1.67 us
  transfers between devices with their start and end apart: 22, of which 8 were waited for; matrix products, arithmetic and copies ran while one was open for 0% of the time, Pallas kernels for 26%

profile of v1, /device:TPU:0, one launch (start us, length us, event | category | flops | bytes accessed | tf_op | source)
XLA Modules:
  0.0 77.0 jit_solution(6270896643428335568)
XLA Ops:
  0.7 1.4 %copy-done.5 = bf16[128,4096]{1,0:T(8,128)(2,1)S(1)} copy-done((bf16[128,4096]{1,0:T(8,128)(2,1)S(1)}, bf16[128,4096]{1,0:T(8,128)(2,1)}, u32[]{:S(2)}) %copy-start.5) | copy-done | bytes 1048600
  2.0 1.0 %copy-done.6 = bf16[4096]{0:T(1024)(128)(2,1)S(1)} copy-done((bf16[4096]{0:T(1024)(128)(2,1)S(1)}, bf16[4096]{0:T(1024)(128)(2,1)}, u32[]{:S(2)}) %copy-start.6) | copy-done | bytes 8216
  3.0 0.7 norm_columns.1
  3.7 0.0 copy-start.1
  3.7 0.0 copy-start.4
  3.7 0.8 %query_part.1 = (f32[128,512]{1,0:T(8,128)S(1)}, bf16[128,512]{1,0:T(8,128)(2,1)S(1)}, bf16[2,64,512]{2,1,0:T(8,128)(2,1)S(1)}, bf16[64,512]{1,0:T(8,128)(2,1)S(1)}) custom-call(bf16[128,4096]{1,0:T(8,128)(2,1)S(1)} %get-tuple-element.50.hn, bf16[2048,1024]{1,0:T(8,128)(2,1)S(1)} %copy-done, bf16[128,1024]{1,0:T(8,128)(2,1)S(1)} %copy-done.3), custom_call_target="tpu_custom_call" | custom-call | tf_op jit(solution)/shard_map/query_part/pallas_call | solution.py:38
  4.6 3.0 %collective-permute-start = (bf16[128,512]{1,0:T(8,128)(2,1)S(1)}, bf16[128,512]{1,0:T(8,128)(2,1)S(1)}, u32[]{:S(2)}, u32[]{:S(2)}) collective-permute-start(bf16[128,512]{1,0:T(8,128)(2,1)S(1)} %get-tuple-element.54), channel_id=1, source_target_pairs={{0,16},{16,0},{1,17},{17,1},{2,18},{18,2},{3,19},{19,3},{4,20},{20... | collective-permute-start | bytes 393224 | tf_op jit(solution)/shard_map/ppermute | solution.py:56
  7.6 1.3 %collective-permute-start.1 = (bf16[2,64,512]{2,1,0:T(8,128)(2,1)S(1)}, bf16[2,64,512]{2,1,0:T(8,128)(2,1)S(1)}, u32[]{:S(2)}, u32[]{:S(2)}) collective-permute-start(bf16[2,64,512]{2,1,0:T(8,128)(2,1)S(1)} %get-tuple-element.55), channel_id=1, source_target_pairs={{2,0},{4,2},{6,4},{8,6},{10,8},{12,10},{14,12},{3,1},{5,3},{7,5},{... | collective-permute-start | bytes 393224 | tf_op jit(solution)/shard_map/ppermute | solution.py:552
  8.9 1.3 %collective-permute-start.2 = (bf16[64,512]{1,0:T(8,128)(2,1)S(1)}, bf16[64,512]{1,0:T(8,128)(2,1)S(1)}, u32[]{:S(2)}, u32[]{:S(2)}) collective-permute-start(bf16[64,512]{1,0:T(8,128)(2,1)S(1)} %get-tuple-element.56), channel_id=1, source_target_pairs={{2,16},{4,18},{6,20},{8,22},{10,24},{12,26},{14,28},{18,0},{20,2},... | collective-permute-start | bytes 196616 | tf_op jit(solution)/shard_map/ppermute | solution.py:553
  10.2 5.7 %collective-permute-start.6 = (bf16[1,2,512,128]{3,2,1,0:T(8,128)(2,1)S(1)}, bf16[1,2,512,128]{3,2,1,0:T(8,128)(2,1)S(1)}, u32[]{:S(2)}, u32[]{:S(2)}) collective-permute-start(bf16[1,2,512,128]{3,2,1,0:T(8,128)(2,1)S(1)} %get-tuple-element.70), channel_id=1, source_target_pairs={{0,8},{2,10},{4,12},{6,14},{8,0},{10,2},{12,4},{14,6},{1,9},{3,11}... | collective-permute-start | bytes 786440 | tf_op jit(solution)/shard_map/ppermute | solution.py:56
  15.9 0.0 copy-start.8
  16.0 5.3 %pool_project.1 = (bf16[2,2048,512]{2,1,0:T(8,128)(2,1)S(1)}, bf16[896,2048]{1,0:T(8,128)(2,1)S(1)}) custom-call(bf16[896]{0:T(1024)(128)(2,1)S(1)} %copy-done.4, bf16[2048,896]{1,0:T(8,128)(2,1)S(1)} %bitcast.2, bf16[2,896,1024]{2,1,0:T(8,128)(2,1)S(1)} %copy-done.2), custom_call_target="tpu_custom_call" | custom-call | tf_op jit(solution)/shard_map/pool_project/pallas_call | solution.py:38
  21.2 0.0 collective-permute-done.2.cross
  21.3 4.8 %attend.1 = (bf16[128,512]{1,0:T(8,128)(2,1)S(1)}, bf16[128,128]{1,0:T(8,128)(2,1)S(1)}, bf16[64,640]{1,0:T(8,128)(2,1)S(1)}, bf16[512,2048]{1,0:T(8,128)(2,1)S(1)}, bf16[512,2048]{1,0:T(8,128)(2,1)S(1)}) custom-call(s32[2,16]{1,0:T(2,128)S(1)} %copy-done.7, s32[2]{0:T(128)S(1)} %copy-done.8, f32[128,512]{1,0:T(8,128)S(1)} %get-tuple-element.53.keep, ...), custom_call_target="tpu_custom_call" | custom-call | flops 4000000000 | tf_op jit(solution)/shard_map/attend/pallas_call | solution.py:38
  26.1 3.6 %collective-permute-start.3 = (bf16[64,640]{1,0:T(8,128)(2,1)S(1)}, bf16[64,640]{1,0:T(8,128)(2,1)S(1)}, u32[]{:S(2)}, u32[]{:S(2)}) collective-permute-start(bf16[64,640]{1,0:T(8,128)(2,1)S(1)} %get-tuple-element.60), channel_id=1, source_target_pairs={{0,2},{2,4},{4,6},{6,8},{8,10},{10,12},{12,14},{1,3},{3,5},{5,7},{... | collective-permute-start | bytes 245768 | tf_op jit(solution)/shard_map/ppermute | solution.py:579
  29.7 2.2 %kv_part_0.1 = (bf16[4,2,56,512]{3,2,1,0:T(8,128)(2,1)S(1)}, f32[4,2,56,512]{3,2,1,0:T(8,128)S(1)}) custom-call(bf16[896,2048]{1,0:T(8,128)(2,1)S(1)} %get-tuple-element.52.turned, bf16[512,2048]{1,0:T(8,128)(2,1)S(1)} %get-tuple-element.80.turned_kv), custom_call_target="tpu_custom_call" | custom-call | tf_op jit(solution)/shard_map/kv_part_0/pallas_call | solution.py:38
  31.9 1.6 %collective-permute-start.15 = (bf16[4,2,56,512]{3,2,1,0:T(8,128)(2,1)S(1)}, bf16[4,2,56,512]{3,2,1,0:T(8,128)(2,1)S(1)}, u32[]{:S(2)}, u32[]{:S(2)}) collective-permute-start(bf16[4,2,56,512]{3,2,1,0:T(8,128)(2,1)S(1)} %get-tuple-element.82), channel_id=1, source_target_pairs={{0,2},{2,0},{4,6},{6,4},{8,10},{10,8},{12,14},{14,12},{1,3},{3,1},... | collective-permute-start | bytes 1376264 | tf_op jit(solution)/shard_map/ppermute | solution.py:56
  33.5 2.2 %kv_part_1.1 = (bf16[2,2,56,512]{3,2,1,0:T(8,128)(2,1)S(1)}, f32[2,2,56,512]{3,2,1,0:T(8,128)S(1)}, bf16[2,2,56,512]{3,2,1,0:T(8,128)(2,1)S(1)}, f32[2,2,56,512]{3,2,1,0:T(8,128)S(1)}) custom-call(bf16[896,2048]{1,0:T(8,128)(2,1)S(1)} %get-tuple-element.52.turned, bf16[512,2048]{1,0:T(8,128)(2,1)S(1)} %get-tuple-element.84.turned_kv), custom_call_target="tpu_custom_call" | custom-call | tf_op jit(solution)/shard_map/kv_part_1/pallas_call | solution.py:38
  35.8 3.2 %collective-permute-start.7 = (bf16[2,1,512,128]{3,2,1,0:T(8,128)(2,1)S(1)}, bf16[2,1,512,128]{3,2,1,0:T(8,128)(2,1)S(1)}, u32[]{:S(2)}, u32[]{:S(2)}) collective-permute-start(bf16[2,1,512,128]{3,2,1,0:T(8,128)(2,1)S(1)} %get-tuple-element.72), channel_id=1, source_target_pairs={{0,4},{2,6},{4,0},{6,2},{8,12},{10,14},{12,8},{14,10},{1,5},{3,7},... | collective-permute-start | bytes 786440 | tf_op jit(solution)/shard_map/ppermute | solution.py:56
  39.1 2.1 %collective-permute-start.17 = (bf16[2,2,56,512]{3,2,1,0:T(8,128)(2,1)S(1)}, bf16[2,2,56,512]{3,2,1,0:T(8,128)(2,1)S(1)}, u32[]{:S(2)}, u32[]{:S(2)}) collective-permute-start(bf16[2,2,56,512]{3,2,1,0:T(8,128)(2,1)S(1)} %get-tuple-element.89), channel_id=1, source_target_pairs={{0,2},{2,0},{4,6},{6,4},{8,10},{10,8},{12,14},{14,12},{1,3},{3,1},... | collective-permute-start | bytes 688136 | tf_op jit(solution)/shard_map/ppermute | solution.py:56
  41.1 0.5 collective-permute-start.4
  41.6 2.3 %collective-permute-done.7.refs_1_ = bf16[2,1,512,128]{3,2,1,0:T(8,128)(2,1)S(1)} collective-permute-done((bf16[2,1,512,128]{3,2,1,0:T(8,128)(2,1)S(1)}, bf16[2,1,512,128]{3,2,1,0:T(8,128)(2,1)S(1)}, u32[]{:S(2)}, u32[]{:S(2)}) %collective-permute-start.7) | collective-permute-done | bytes 262176 | tf_op jit(solution)/shard_map/ppermute | solution.py:56
  43.9 4.0 %collective-permute-done.10.refs_1_.refs_5_ = bf16[1,128,512]{2,1,0:T(8,128)(2,1)S(1)} collective-permute-done((bf16[1,128,512]{2,1,0:T(8,128)(2,1)S(1)}, bf16[1,128,512]{2,1,0:T(8,128)(2,1)S(1)}, u32[]{:S(2)}, u32[]{:S(2)}) %collective-permute-start.10) | collective-permute-done | bytes 131104 | tf_op jit(solution)/shard_map/ppermute | solution.py:56
  48.0 0.1 collective-permute-start.11
  48.1 0.1 collective-permute-start.9
  48.2 0.1 odd_sums.1
  48.3 2.0 %collective-permute-start.18 = (bf16[2,2,2,56,512]{4,3,2,1,0:T(8,128)(2,1)S(1)}, bf16[2,2,2,56,512]{4,3,2,1,0:T(8,128)(2,1)S(1)}, u32[]{:S(2)}, u32[]{:S(2)}) collective-permute-start(bf16[2,2,2,56,512]{4,3,2,1,0:T(8,128)(2,1)S(1)} %odd_sums.1), channel_id=1, source_target_pairs={{0,4},{2,6},{4,0},{6,2},{8,12},{10,14},{12,8},{14,10},{1,5},{3,7},... | collective-permute-start | bytes 1376264 | tf_op jit(solution)/shard_map/ppermute | solution.py:56
  50.3 0.6 collective-permute-start.16
  50.8 1.6 %normed_part.1 = (f32[128,1024]{1,0:T(8,128)S(1)}, f32[128,1]{1,0:T(8,128)S(1)}, bf16[128,1152]{1,0:T(8,128)(2,1)S(1)}) custom-call(bf16[128,640]{1,0:T(8,128)(2,1)S(1)} %get-tuple-element.61.own, bf16[128,640]{1,0:T(8,128)(2,1)S(1)} %collective-permute-done.4.other, bf16[2048,1024]{1,0:T(8,128)(2,1)S(1)} %copy-done), custom_call_target="tpu_custom_call" | custom-call | tf_op jit(solution)/shard_map/normed_part/pallas_call | solution.py:38
  52.4 0.1 collective-permute-start.5
  52.5 4.7 %collective-permute-done.11.refs_6_ = bf16[2,128,512]{2,1,0:T(8,128)(2,1)S(1)} collective-permute-done((bf16[2,128,512]{2,1,0:T(8,128)(2,1)S(1)}, bf16[2,128,512]{2,1,0:T(8,128)(2,1)S(1)}, u32[]{:S(2)}, u32[]{:S(2)}) %collective-permute-start.11) | collective-permute-done | bytes 262176 | tf_op jit(solution)/shard_map/ppermute | solution.py:56
  57.2 1.2 %weight_part.1 = (f32[256,512]{1,0:T(8,128)S(1)}, bf16[256,512]{1,0:T(8,128)(2,1)S(1)}, bf16[256,512]{1,0:T(8,128)(2,1)S(1)}, bf16[256,512]{1,0:T(8,128)(2,1)S(1)}) custom-call(bf16[2,1,512,128]{3,2,1,0:T(8,128)(2,1)S(1)} %get-tuple-element.71.refs_0_, bf16[2,1,512,128]{3,2,1,0:T(8,128)(2,1)S(1)} %collective-permute-done.7.refs_1_, ...), custom_call_target="tpu_custom_call" | custom-call | tf_op jit(solution)/shard_map/weight_part/pallas_call | solution.py:38
  58.5 0.1 collective-permute-start.12
  58.5 1.2 %collective-permute-start.13 = (bf16[256,512]{1,0:T(8,128)(2,1)S(1)}, bf16[256,512]{1,0:T(8,128)(2,1)S(1)}, u32[]{:S(2)}, u32[]{:S(2)}) collective-permute-start(bf16[256,512]{1,0:T(8,128)(2,1)S(1)} %get-tuple-element.77), channel_id=1, source_target_pairs={{0,18},{2,16},{4,22},{6,20},{8,26},{10,24},{12,30},{14,28},{16,2},... | collective-permute-start | bytes 786440 | tf_op jit(solution)/shard_map/ppermute | solution.py:567
  59.7 2.3 %collective-permute-start.14 = (bf16[256,512]{1,0:T(8,128)(2,1)S(1)}, bf16[256,512]{1,0:T(8,128)(2,1)S(1)}, u32[]{:S(2)}, u32[]{:S(2)}) collective-permute-start(bf16[256,512]{1,0:T(8,128)(2,1)S(1)} %get-tuple-element.78), channel_id=1, source_target_pairs={{0,16},{16,0},{1,17},{17,1},{2,18},{18,2},{3,19},{19,3},{4,20},{20... | collective-permute-start | bytes 786440 | tf_op jit(solution)/shard_map/ppermute | solution.py:56
  62.0 0.1 even_sums.1.kept
  62.1 2.1 %collective-permute-done.18.received = bf16[2,2,2,56,512]{4,3,2,1,0:T(8,128)(2,1)S(1)} collective-permute-done((bf16[2,2,2,56,512]{4,3,2,1,0:T(8,128)(2,1)S(1)}, bf16[2,2,2,56,512]{4,3,2,1,0:T(8,128)(2,1)S(1)}, u32[]{:S(2)}, u32[]{:S(2)}) %collective-permute-start.18) | collective-permute-done | bytes 458784 | tf_op jit(solution)/shard_map/ppermute | solution.py:56
  64.2 0.1 outer_sums.1
  64.3 0.1 collective-permute-start.19
  64.4 2.8 %collective-permute-start.20 = (bf16[2,56,512]{2,1,0:T(8,128)(2,1)S(1)}, bf16[2,56,512]{2,1,0:T(8,128)(2,1)S(1)}, u32[]{:S(2)}, u32[]{:S(2)}) collective-permute-start(bf16[2,56,512]{2,1,0:T(8,128)(2,1)S(1)} %get-tuple-element.93), channel_id=1, source_target_pairs={{0,24},{2,26},{4,28},{6,30},{8,16},{10,18},{12,20},{14,22},{16,8},... | collective-permute-start | bytes 344072 | tf_op jit(solution)/shard_map/ppermute | solution.py:567
  67.2 1.6 %collective-permute-start.21 = (bf16[2,56,512]{2,1,0:T(8,128)(2,1)S(1)}, bf16[2,56,512]{2,1,0:T(8,128)(2,1)S(1)}, u32[]{:S(2)}, u32[]{:S(2)}) collective-permute-start(bf16[2,56,512]{2,1,0:T(8,128)(2,1)S(1)} %get-tuple-element.94), channel_id=1, source_target_pairs={{0,16},{16,0},{1,17},{17,1},{2,18},{18,2},{3,19},{19,3},{4,20},{20... | collective-permute-start | bytes 344072 | tf_op jit(solution)/shard_map/ppermute | solution.py:56
  68.8 1.0 %hidden_grad.1 = (bf16[128,1024]{1,0:T(8,128)(2,1)}, f32[1,128]{1,0:T(1,128)}) custom-call(f32[128,1024]{1,0:T(8,128)S(1)} %get-tuple-element.62.kept, bf16[128,1152]{1,0:T(8,128)(2,1)S(1)} %collective-permute-done.5.received, f32[128,1]{1,0:T(8,128)S(1)} %get-tuple-element.64.dots, bf16[128,1024]{1,0:T(8,128)(2,1)S(1)} %get-tuple-element.65.hidden, ...), custom_call_target="tpu_custom_call" | custom-call | tf_op jit(solution)/shard_map/hidden_grad/pallas_call | solution.py:38
  69.8 0.3 collective-permute-done.13.cross
  70.1 3.2 %collective-permute-done.14.side = bf16[256,512]{1,0:T(8,128)(2,1)S(1)} collective-permute-done((bf16[256,512]{1,0:T(8,128)(2,1)S(1)}, bf16[256,512]{1,0:T(8,128)(2,1)S(1)}, u32[]{:S(2)}, u32[]{:S(2)}) %collective-permute-start.14) | collective-permute-done | bytes 262176 | tf_op jit(solution)/shard_map/ppermute | solution.py:56
  73.2 1.1 %query_grad.1 = f32[256,1024]{1,0:T(8,128)} custom-call(f32[256,512]{1,0:T(8,128)S(1)} %get-tuple-element.75.kept, bf16[256,512]{1,0:T(8,128)(2,1)S(1)} %collective-permute-done.12.paired, bf16[256,512]{1,0:T(8,128)(2,1)S(1)} %collective-permute-done.13.cross, bf16[256,512]{1,0:T(8,128)(2,1)S(1)} %collective-permute-done.14.side), custom_call_target="tpu_custom_call" | custom-call | tf_op jit(solution)/shard_map/query_grad/pallas_call | solution.py:38
  74.3 1.4 %collective-permute-done.20.cross = bf16[2,56,512]{2,1,0:T(8,128)(2,1)S(1)} collective-permute-done((bf16[2,56,512]{2,1,0:T(8,128)(2,1)S(1)}, bf16[2,56,512]{2,1,0:T(8,128)(2,1)S(1)}, u32[]{:S(2)}, u32[]{:S(2)}) %collective-permute-start.20) | collective-permute-done | bytes 114720 | tf_op jit(solution)/shard_map/ppermute | solution.py:567
  75.7 0.5 collective-permute-done.21.side
  76.1 0.8 %kv_grad.1 = f32[2,56,1024]{2,1,0:T(8,128)} custom-call(f32[2,56,512]{2,1,0:T(8,128)S(1)} %get-tuple-element.91.mine, bf16[2,56,512]{2,1,0:T(8,128)(2,1)S(1)} %collective-permute-done.19.following, bf16[2,56,512]{2,1,0:T(8,128)(2,1)S(1)} %collective-permute-done.20.cross, bf16[2,56,512]{2,1,0:T(8,128)(2,1)S(1)} %collective-permute-done.21.side), custom_call_target="tpu_custom_call" | custom-call | tf_op jit(solution)/shard_map/kv_grad/pallas_call | solution.py:38
  (31 shorter events, 0.1 us)
Async XLA Ops:
  0.6 3.1 %copy-start = (bf16[2048,1024]{1,0:T(8,128)(2,1)S(1)}, bf16[2048,1024]{1,0:T(8,128)(2,1)}, u32[]{:S(2)}) copy-start(bf16[2048,1024]{1,0:T(8,128)(2,1)} %weight.5) | copy-start | bytes 12582916
  0.6 3.1 %copy-start.3 = (bf16[128,1024]{1,0:T(8,128)(2,1)S(1)}, bf16[128,1024]{1,0:T(8,128)(2,1)}, u32[]{:S(2)}) copy-start(bf16[128,1024]{1,0:T(8,128)(2,1)} %grad_own.1) | copy-start | bytes 786436
  0.7 1.4 %copy-start.5 = (bf16[128,4096]{1,0:T(8,128)(2,1)S(1)}, bf16[128,4096]{1,0:T(8,128)(2,1)}, u32[]{:S(2)}) copy-start(bf16[128,4096]{1,0:T(8,128)(2,1)} %hidden.1) | copy-start | bytes 3145732
  2.0 1.0 %copy-start.6 = (bf16[4096]{0:T(1024)(128)(2,1)S(1)}, bf16[4096]{0:T(1024)(128)(2,1)}, u32[]{:S(2)}) copy-start(bf16[4096]{0:T(1024)(128)(2,1)} %gain.2) | copy-start | bytes 24580
  3.0 12.9 %copy-start.2 = (bf16[2,896,1024]{2,1,0:T(8,128)(2,1)S(1)}, bf16[2,896,1024]{2,1,0:T(8,128)(2,1)}, u32[]{:S(2)}) copy-start(bf16[2,896,1024]{2,1,0:T(8,128)(2,1)} %weight.4) | copy-start | bytes 11010052
  3.7 12.2 %copy-start.1 = (bf16[16,128,896]{2,1,0:T(8,128)(2,1)S(1)}, bf16[16,128,896]{2,1,0:T(8,128)(2,1)}, u32[]{:S(2)}) copy-start(bf16[16,128,896]{2,1,0:T(8,128)(2,1)} %param.11) | copy-start | bytes 11010052
  3.7 12.2 %copy-start.4 = (bf16[896]{0:T(1024)(128)(2,1)S(1)}, bf16[896]{0:T(1024)(128)(2,1)}, u32[]{:S(2)}) copy-start(bf16[896]{0:T(1024)(128)(2,1)} %gain.3) | copy-start | bytes 5380
  4.6 16.7 %collective-permute-start = (bf16[128,512]{1,0:T(8,128)(2,1)S(1)}, bf16[128,512]{1,0:T(8,128)(2,1)S(1)}, u32[]{:S(2)}, u32[]{:S(2)}) collective-permute-start(bf16[128,512]{1,0:T(8,128)(2,1)S(1)} %get-tuple-element.54), channel_id=1, source_target_pairs={{0,16},{16,0},{1,17},{17,1},{2,18},{18,2},{3,19},{19,3},{4,20},{20... | collective-permute-start | bytes 393224 | tf_op jit(solution)/shard_map/ppermute | solution.py:56
  7.6 13.7 %collective-permute-start.1 = (bf16[2,64,512]{2,1,0:T(8,128)(2,1)S(1)}, bf16[2,64,512]{2,1,0:T(8,128)(2,1)S(1)}, u32[]{:S(2)}, u32[]{:S(2)}) collective-permute-start(bf16[2,64,512]{2,1,0:T(8,128)(2,1)S(1)} %get-tuple-element.55), channel_id=1, source_target_pairs={{2,0},{4,2},{6,4},{8,6},{10,8},{12,10},{14,12},{3,1},{5,3},{7,5},{... | collective-permute-start | bytes 393224 | tf_op jit(solution)/shard_map/ppermute | solution.py:552
  8.9 12.3 %collective-permute-start.2 = (bf16[64,512]{1,0:T(8,128)(2,1)S(1)}, bf16[64,512]{1,0:T(8,128)(2,1)S(1)}, u32[]{:S(2)}, u32[]{:S(2)}) collective-permute-start(bf16[64,512]{1,0:T(8,128)(2,1)S(1)} %get-tuple-element.56), channel_id=1, source_target_pairs={{2,16},{4,18},{6,20},{8,22},{10,24},{12,26},{14,28},{18,0},{20,2},... | collective-permute-start | bytes 196616 | tf_op jit(solution)/shard_map/ppermute | solution.py:553
  10.2 25.6 %collective-permute-start.6 = (bf16[1,2,512,128]{3,2,1,0:T(8,128)(2,1)S(1)}, bf16[1,2,512,128]{3,2,1,0:T(8,128)(2,1)S(1)}, u32[]{:S(2)}, u32[]{:S(2)}) collective-permute-start(bf16[1,2,512,128]{3,2,1,0:T(8,128)(2,1)S(1)} %get-tuple-element.70), channel_id=1, source_target_pairs={{0,8},{2,10},{4,12},{6,14},{8,0},{10,2},{12,4},{14,6},{1,9},{3,11}... | collective-permute-start | bytes 786440 | tf_op jit(solution)/shard_map/ppermute | solution.py:56
  15.9 5.3 %copy-start.7 = (s32[2,16]{1,0:T(2,128)S(1)}, s32[2,16]{1,0:T(2,128)}, u32[]{:S(2)}) copy-start(s32[2,16]{1,0:T(2,128)} %ids.1) | copy-start | bytes 388
  15.9 5.3 %copy-start.8 = (s32[2]{0:T(128)S(1)}, s32[2]{0:T(128)}, u32[]{:S(2)}) copy-start(s32[2]{0:T(128)} %counts.1) | copy-start | bytes 28
  26.1 12.9 %collective-permute-start.3 = (bf16[64,640]{1,0:T(8,128)(2,1)S(1)}, bf16[64,640]{1,0:T(8,128)(2,1)S(1)}, u32[]{:S(2)}, u32[]{:S(2)}) collective-permute-start(bf16[64,640]{1,0:T(8,128)(2,1)S(1)} %get-tuple-element.60), channel_id=1, source_target_pairs={{0,2},{2,4},{4,6},{6,8},{8,10},{10,12},{12,14},{1,3},{3,5},{5,7},{... | collective-permute-start | bytes 245768 | tf_op jit(solution)/shard_map/ppermute | solution.py:579
  31.9 16.2 %collective-permute-start.15 = (bf16[4,2,56,512]{3,2,1,0:T(8,128)(2,1)S(1)}, bf16[4,2,56,512]{3,2,1,0:T(8,128)(2,1)S(1)}, u32[]{:S(2)}, u32[]{:S(2)}) collective-permute-start(bf16[4,2,56,512]{3,2,1,0:T(8,128)(2,1)S(1)} %get-tuple-element.82), channel_id=1, source_target_pairs={{0,2},{2,0},{4,6},{6,4},{8,10},{10,8},{12,14},{14,12},{1,3},{3,1},... | collective-permute-start | bytes 1376264 | tf_op jit(solution)/shard_map/ppermute | solution.py:56
  35.8 8.1 %collective-permute-start.7 = (bf16[2,1,512,128]{3,2,1,0:T(8,128)(2,1)S(1)}, bf16[2,1,512,128]{3,2,1,0:T(8,128)(2,1)S(1)}, u32[]{:S(2)}, u32[]{:S(2)}) collective-permute-start(bf16[2,1,512,128]{3,2,1,0:T(8,128)(2,1)S(1)} %get-tuple-element.72), channel_id=1, source_target_pairs={{0,4},{2,6},{4,0},{6,2},{8,12},{10,14},{12,8},{14,10},{1,5},{3,7},... | collective-permute-start | bytes 786440 | tf_op jit(solution)/shard_map/ppermute | solution.py:56
  39.1 9.0 %collective-permute-start.17 = (bf16[2,2,56,512]{3,2,1,0:T(8,128)(2,1)S(1)}, bf16[2,2,56,512]{3,2,1,0:T(8,128)(2,1)S(1)}, u32[]{:S(2)}, u32[]{:S(2)}) collective-permute-start(bf16[2,2,56,512]{3,2,1,0:T(8,128)(2,1)S(1)} %get-tuple-element.89), channel_id=1, source_target_pairs={{0,2},{2,0},{4,6},{6,4},{8,10},{10,8},{12,14},{14,12},{1,3},{3,1},... | collective-permute-start | bytes 688136 | tf_op jit(solution)/shard_map/ppermute | solution.py:56
  41.1 6.8 %collective-permute-start.10 = (bf16[1,128,512]{2,1,0:T(8,128)(2,1)S(1)}, bf16[1,128,512]{2,1,0:T(8,128)(2,1)S(1)}, u32[]{:S(2)}, u32[]{:S(2)}) collective-permute-start(bf16[1,128,512]{2,1,0:T(8,128)(2,1)S(1)} %get-tuple-element.74.refs_0_.refs_4_), channel_id=1, source_target_pairs={{0,8},{2,10},{4,12},{6,14},{8,0},{10,2},{12,4},{14,6},{1,9},{3,11}... | collective-permute-start | bytes 393224 | tf_op jit(solution)/shard_map/ppermute | solution.py:56
  41.1 9.1 %collective-permute-start.4 = (bf16[128,640]{1,0:T(8,128)(2,1)S(1)}, bf16[128,640]{1,0:T(8,128)(2,1)S(1)}, u32[]{:S(2)}, u32[]{:S(2)}) collective-permute-start(bf16[128,640]{1,0:T(8,128)(2,1)S(1)} %get-tuple-element.61.own), channel_id=1, source_target_pairs={{0,16},{16,0},{1,17},{17,1},{2,18},{18,2},{3,19},{19,3},{4,20},{20... | collective-permute-start | bytes 491528 | tf_op jit(solution)/shard_map/ppermute | solution.py:56
  43.9 8.5 %collective-permute-start.8 = (bf16[2,1,512,128]{3,2,1,0:T(8,128)(2,1)S(1)}, bf16[2,1,512,128]{3,2,1,0:T(8,128)(2,1)S(1)}, u32[]{:S(2)}, u32[]{:S(2)}) collective-permute-start(bf16[2,1,512,128]{3,2,1,0:T(8,128)(2,1)S(1)} %get-tuple-element.71.refs_0_), channel_id=1, source_target_pairs={{0,1},{1,0},{2,3},{3,2},{4,5},{5,4},{6,7},{7,6},{8,9},{9,8},{10,11... | collective-permute-start | bytes 786440 | tf_op jit(solution)/shard_map/ppermute | solution.py:56
  48.0 9.2 %collective-permute-start.11 = (bf16[2,128,512]{2,1,0:T(8,128)(2,1)S(1)}, bf16[2,128,512]{2,1,0:T(8,128)(2,1)S(1)}, u32[]{:S(2)}, u32[]{:S(2)}) collective-permute-start(bf16[2,128,512]{2,1,0:T(8,128)(2,1)S(1)} %stacked.1), channel_id=1, source_target_pairs={{0,4},{2,6},{4,0},{6,2},{8,12},{10,14},{12,8},{14,10},{1,5},{3,7},... | collective-permute-start | bytes 786440 | tf_op jit(solution)/shard_map/ppermute | solution.py:56
  48.1 9.2 %collective-permute-start.9 = (bf16[2,1,512,128]{3,2,1,0:T(8,128)(2,1)S(1)}, bf16[2,1,512,128]{3,2,1,0:T(8,128)(2,1)S(1)}, u32[]{:S(2)}, u32[]{:S(2)}) collective-permute-start(bf16[2,1,512,128]{3,2,1,0:T(8,128)(2,1)S(1)} %collective-permute-done.7.refs_1_), channel_id=1, source_target_pairs={{0,1},{1,0},{2,3},{3,2},{4,5},{5,4},{6,7},{7,6},{8,9},{9,8},{10,11... | collective-permute-start | bytes 786440 | tf_op jit(solution)/shard_map/ppermute | solution.py:56
  48.3 16.0 %collective-permute-start.18 = (bf16[2,2,2,56,512]{4,3,2,1,0:T(8,128)(2,1)S(1)}, bf16[2,2,2,56,512]{4,3,2,1,0:T(8,128)(2,1)S(1)}, u32[]{:S(2)}, u32[]{:S(2)}) collective-permute-start(bf16[2,2,2,56,512]{4,3,2,1,0:T(8,128)(2,1)S(1)} %odd_sums.1), channel_id=1, source_target_pairs={{0,4},{2,6},{4,0},{6,2},{8,12},{10,14},{12,8},{14,10},{1,5},{3,7},... | collective-permute-start | bytes 1376264 | tf_op jit(solution)/shard_map/ppermute | solution.py:56
  50.3 9.5 %collective-permute-start.16 = (bf16[2,2,56,512]{3,2,1,0:T(8,128)(2,1)S(1)}, bf16[2,2,56,512]{3,2,1,0:T(8,128)(2,1)S(1)}, u32[]{:S(2)}, u32[]{:S(2)}) collective-permute-start(bf16[2,2,56,512]{3,2,1,0:T(8,128)(2,1)S(1)} %get-tuple-element.86), channel_id=1, source_target_pairs={{0,2},{2,0},{4,6},{6,4},{8,10},{10,8},{12,14},{14,12},{1,3},{3,1},... | collective-permute-start | bytes 688136 | tf_op jit(solution)/shard_map/ppermute | solution.py:56
  52.4 12.0 %collective-permute-start.5 = (bf16[128,1152]{1,0:T(8,128)(2,1)S(1)}, bf16[128,1152]{1,0:T(8,128)(2,1)S(1)}, u32[]{:S(2)}, u32[]{:S(2)}) collective-permute-start(bf16[128,1152]{1,0:T(8,128)(2,1)S(1)} %get-tuple-element.63), channel_id=1, source_target_pairs={{0,1},{1,0},{2,3},{3,2},{4,5},{5,4},{6,7},{7,6},{8,9},{9,8},{10,11... | collective-permute-start | bytes 884744 | tf_op jit(solution)/shard_map/ppermute | solution.py:56
  58.5 8.7 %collective-permute-start.12 = (bf16[256,512]{1,0:T(8,128)(2,1)S(1)}, bf16[256,512]{1,0:T(8,128)(2,1)S(1)}, u32[]{:S(2)}, u32[]{:S(2)}) collective-permute-start(bf16[256,512]{1,0:T(8,128)(2,1)S(1)} %get-tuple-element.76), channel_id=1, source_target_pairs={{0,2},{2,0},{4,6},{6,4},{8,10},{10,8},{12,14},{14,12},{1,3},{3,1},... | collective-permute-start | bytes 786440 | tf_op jit(solution)/shard_map/ppermute | solution.py:56
  58.5 11.5 %collective-permute-start.13 = (bf16[256,512]{1,0:T(8,128)(2,1)S(1)}, bf16[256,512]{1,0:T(8,128)(2,1)S(1)}, u32[]{:S(2)}, u32[]{:S(2)}) collective-permute-start(bf16[256,512]{1,0:T(8,128)(2,1)S(1)} %get-tuple-element.77), channel_id=1, source_target_pairs={{0,18},{2,16},{4,22},{6,20},{8,26},{10,24},{12,30},{14,28},{16,2},... | collective-permute-start | bytes 786440 | tf_op jit(solution)/shard_map/ppermute | solution.py:567
  59.7 13.5 %collective-permute-start.14 = (bf16[256,512]{1,0:T(8,128)(2,1)S(1)}, bf16[256,512]{1,0:T(8,128)(2,1)S(1)}, u32[]{:S(2)}, u32[]{:S(2)}) collective-permute-start(bf16[256,512]{1,0:T(8,128)(2,1)S(1)} %get-tuple-element.78), channel_id=1, source_target_pairs={{0,16},{16,0},{1,17},{17,1},{2,18},{18,2},{3,19},{19,3},{4,20},{20... | collective-permute-start | bytes 786440 | tf_op jit(solution)/shard_map/ppermute | solution.py:56
  64.3 10.0 %collective-permute-start.19 = (bf16[2,56,512]{2,1,0:T(8,128)(2,1)S(1)}, bf16[2,56,512]{2,1,0:T(8,128)(2,1)S(1)}, u32[]{:S(2)}, u32[]{:S(2)}) collective-permute-start(bf16[2,56,512]{2,1,0:T(8,128)(2,1)S(1)} %get-tuple-element.92), channel_id=1, source_target_pairs={{0,8},{2,10},{4,12},{6,14},{8,0},{10,2},{12,4},{14,6},{1,9},{3,11}... | collective-permute-start | bytes 344072 | tf_op jit(solution)/shard_map/ppermute | solution.py:56
  64.4 11.2 %collective-permute-start.20 = (bf16[2,56,512]{2,1,0:T(8,128)(2,1)S(1)}, bf16[2,56,512]{2,1,0:T(8,128)(2,1)S(1)}, u32[]{:S(2)}, u32[]{:S(2)}) collective-permute-start(bf16[2,56,512]{2,1,0:T(8,128)(2,1)S(1)} %get-tuple-element.93), channel_id=1, source_target_pairs={{0,24},{2,26},{4,28},{6,30},{8,16},{10,18},{12,20},{14,22},{16,8},... | collective-permute-start | bytes 344072 | tf_op jit(solution)/shard_map/ppermute | solution.py:567
  67.2 8.9 %collective-permute-start.21 = (bf16[2,56,512]{2,1,0:T(8,128)(2,1)S(1)}, bf16[2,56,512]{2,1,0:T(8,128)(2,1)S(1)}, u32[]{:S(2)}, u32[]{:S(2)}) collective-permute-start(bf16[2,56,512]{2,1,0:T(8,128)(2,1)S(1)} %get-tuple-element.94), channel_id=1, source_target_pairs={{0,16},{16,0},{1,17},{17,1},{2,18},{18,2},{3,19},{19,3},{4,20},{20... | collective-permute-start | bytes 344072 | tf_op jit(solution)/shard_map/ppermute | solution.py:56
